TPU v7x, 32 devices: a whole 2x2x4 slice. The times are simulated.
32 devices in a mesh: groups: 2 (over y), cls: 4 (over z), rep: 4 (over x, core).
Axes of the slice: x: 2, y: 2, z: 4, core: 2. Of those that a mesh axis runs over, the one named last changes fastest.
Arguments:
- particles: bfloat16 [1024, 256, 256], P(('groups', 'cls', 'rep')), parts along dimension 0, may hold values from -6 to 6
- classes: int32 [1024], P(('groups', 'cls', 'rep')), parts along dimension 0, may hold values from 0 to 23, as said below
- rotation: int32 [1024], P(('groups', 'cls', 'rep')), parts along dimension 0, may hold values from 0 to 7
- defocus: int32 [1024], P(('groups', 'cls', 'rep')), parts along dimension 0, may hold values from 0 to 3
- filter_taps: float32 [31], replicated, may hold values from -1 to 1
- ctf_table: bfloat16 [4, 256, 256], replicated, may hold values from -1.01 to 1.01
- references: bfloat16 [48, 256, 256], P(('groups', 'cls'), 'rep'), parts along dimension 0, may hold values from -6 to 6
Outputs:
- new_references: float32 [48, 256, 256], P(('groups', 'cls'), 'rep'), parts along dimension 0
There are 2 independent parts, one for each index of `groups`. A program takes and returns all parts, laid end to end along the dimension named above; an argument that names none is the same for every part. Nothing has to cross between parts.
Inputs may be any that keep to these rules, and one draw needn't show every extreme that they name: Among the 32 particles of one device (aligned blocks of 32 rows in order), at most 16 are assigned to classes of one index o of cls, the classes o * 6 to o * 6 + 5; in every such block some index receives exactly 16.
All inputs are finite; a program needn't handle non-finite values.
Results may differ from a plain program's by a relative error of at most 0.0065.
Values may be sent and summed in bfloat16 or wider, within the bound.
A program may use at most 64 MiB of HBM per device.

v0:
```python
import math

import jax
import jax.numpy as jnp
from jax import lax
from jax.sharding import PartitionSpec as P

EPSILON = 1e-05
PRIOR_WEIGHT = 4.0


def hartley_table(tile_len):
    pixel_index = jnp.arange(tile_len, dtype=jnp.int32)
    product = pixel_index[:, None] * pixel_index[None, :] % tile_len
    phases = 2.0 * math.pi / tile_len * product.astype(jnp.float32)
    return jnp.cos(phases) + jnp.sin(phases)


def band_table(filter_taps, tile_len):
    half_width = (filter_taps.shape[0] - 1) // 2
    matrix = jnp.zeros((tile_len, tile_len), jnp.float32)
    for offset in range(filter_taps.shape[0]):
        matrix = matrix + filter_taps[offset] * jnp.eye(
            tile_len, k=offset - half_width, dtype=jnp.float32
        )
    return matrix


def orient(tile_block, turn_codes):
    transpose_mask = (turn_codes >= 4)[:, None, None]
    flip_rows = (turn_codes % 2 == 1)[:, None, None]
    flip_cols = (turn_codes // 2 % 2 == 1)[:, None, None]
    turned = jnp.where(transpose_mask, jnp.swapaxes(tile_block, 1, 2), tile_block)
    turned = jnp.where(flip_rows, turned[:, ::-1, :], turned)
    return jnp.where(flip_cols, turned[:, :, ::-1], turned)


def local(particles, classes, rotation, defocus, filter_taps, ctf_table, references):
    tile_count = particles.shape[0]
    tile_len = particles.shape[1]
    own_classes = references.shape[0]
    bins_count = ctf_table.shape[0]
    pixel_count = tile_len * tile_len
    owners = lax.axis_size("cls")
    capacity = max(2, (2 * tile_count + owners - 1) // owners)
    slot_count = owners * capacity
    hartley = hartley_table(tile_len)
    analysis = jnp.dot(
        hartley,
        band_table(filter_taps, tile_len),
        preferred_element_type=jnp.float32,
        precision=lax.Precision.HIGHEST,
    ).astype(jnp.bfloat16)
    synthesis = hartley.astype(jnp.bfloat16)
    group_size = math.gcd(tile_count, 8)
    group_count = tile_count // group_size

    def filter_group(inputs):
        tile_block, turn_codes, bin_ids = inputs
        oriented = orient(tile_block, turn_codes)
        bin_hits = (bin_ids[:, None] == jnp.arange(bins_count)[None, :]).astype(jnp.bfloat16)
        spectral_gain = jnp.einsum(
            "pb,bxy->pxy", bin_hits, ctf_table, preferred_element_type=jnp.float32
        )
        first_pass = jnp.einsum(
            "pij,lj->pil", oriented, analysis, preferred_element_type=jnp.float32
        ).astype(jnp.bfloat16)
        raw_spectra = jnp.einsum(
            "li,pim->plm", analysis, first_pass, preferred_element_type=jnp.float32
        )
        spectra = (raw_spectra * spectral_gain).astype(jnp.bfloat16)
        second_pass = jnp.einsum(
            "pkm,my->pky", spectra, synthesis, preferred_element_type=jnp.float32
        ).astype(jnp.bfloat16)
        return (
            jnp.einsum("xk,pky->pxy", synthesis, second_pass, preferred_element_type=jnp.float32)
            / pixel_count
        ).astype(jnp.bfloat16)

    grouped = (
        particles.reshape(group_count, group_size, tile_len, tile_len),
        rotation.reshape(group_count, group_size),
        defocus.reshape(group_count, group_size),
    )
    filtered = lax.map(filter_group, grouped).reshape(tile_count, tile_len, tile_len)
    owner_of = classes // own_classes
    owner_hits = (owner_of[:, None] == jnp.arange(owners)[None, :]).astype(jnp.int32)
    earlier = jnp.cumsum(owner_hits, axis=0) - owner_hits
    position = jnp.sum(earlier * owner_hits, axis=1)
    slot_index = owner_of * capacity + position
    routing = (jnp.arange(slot_count)[:, None] == slot_index[None, :]).astype(jnp.bfloat16)
    outgoing = jnp.einsum(
        "sp,pxy->sxy", routing, filtered, preferred_element_type=jnp.float32
    ).astype(jnp.bfloat16)
    outgoing = outgoing.reshape(owners, capacity, tile_len, tile_len)
    class_hits = ((classes % own_classes)[:, None] == jnp.arange(own_classes)[None, :]).astype(
        jnp.bfloat16
    )
    labels = jnp.dot(routing, class_hits, preferred_element_type=jnp.float32).astype(jnp.bfloat16)
    labels = labels.reshape(owners, capacity, own_classes)
    arrived, membership = (
        lax.all_to_all(outgoing, "cls", split_axis=0, concat_axis=0, tiled=True),
        lax.all_to_all(labels, "cls", split_axis=0, concat_axis=0, tiled=True),
    )
    tile_power = (
        jnp.einsum("sjxy,sjxy->sj", arrived, arrived, preferred_element_type=jnp.float32)
        / pixel_count
    )
    piece = lax.all_gather(references, "rep", axis=1, tiled=True)
    intersections = jnp.einsum("sjxy,kxy->sjk", arrived, piece, preferred_element_type=jnp.float32)
    squares = jnp.einsum("kxy,kxy->k", piece, piece, preferred_element_type=jnp.float32)
    intersections, squares = (intersections, squares)
    member_f = membership.astype(jnp.float32)
    intersection = jnp.sum(member_f * intersections, axis=2) / pixel_count
    ref_power = jnp.sum(member_f * squares[None, None, :], axis=2) / pixel_count
    scores = intersection / jnp.sqrt((tile_power + EPSILON) * (ref_power + EPSILON))
    weight = jax.nn.sigmoid(tile_len * scores)
    scaling = (weight / jnp.sqrt(tile_power + EPSILON)).astype(jnp.bfloat16)
    mixing = membership * scaling[:, :, None]
    class_sums = jnp.einsum("sjk,sjxy->kxy", mixing, arrived, preferred_element_type=jnp.float32)
    class_weights = jnp.sum(member_f * weight[:, :, None], axis=(0, 1))
    row_count = references.shape[1]
    summed, weights_all = (
        lax.psum(class_sums.astype(jnp.bfloat16), "rep").astype(jnp.float32),
        lax.psum(class_weights.astype(jnp.bfloat16), "rep").astype(jnp.float32),
    )
    rep_index = lax.axis_index("rep")
    own_rows = lax.dynamic_slice_in_dim(summed, rep_index * row_count, row_count, 1)
    own_total = weights_all[:, None, None]
    return (PRIOR_WEIGHT * references.astype(jnp.float32) + own_rows) / (PRIOR_WEIGHT + own_total)


def solution(mesh):
    placed = (
        P(("groups", "cls", "rep"), None, None),
        P(("groups", "cls", "rep")),
        P(("groups", "cls", "rep")),
        P(("groups", "cls", "rep")),
        P(),
        P(),
        P(("groups", "cls"), "rep", None),
    )
    return jax.shard_map(
        local,
        mesh=mesh,
        in_specs=placed,
        out_specs=P(("groups", "cls"), "rep", None),
        check_vma=False,
    )
```

profile of v0, /device:TPU:0, one launch (start us, length us, event | category | flops | bytes accessed | tf_op | source)
XLA Modules:
  0.0 437.0 jit_solution(1913934423850431032)
XLA Ops:
  6.5 0.7 and_select_fusion.3
  7.3 0.2 select_reduce_fusion
  7.5 0.3 convolution_convert_fusion.4
  7.9 0.6 copy.42
  8.5 6.3 %all-to-all-start = ((bf16[4,16,6]{1,2,0:T(8,128)(2,1)}), bf16[4,16,6]{1,2,0:T(8,128)(2,1)S(1)}, u32[]{:S(2)}, u32[]{:S(2)}) async-start(bf16[4,16,6]{1,2,0:T(8,128)(2,1)} %copy.42), calls=%async_computation | async-start | bytes 16384 | tf_op jit(solution)/shard_map/all_to_all | solution.py:103
  14.8 2.1 fusion.206
  16.9 1.8 fusion.207
  18.8 2.2 copy.43
  21.1 0.7 reshape.95
  21.8 0.7 reshape.97
  22.5 21.8 %convolution_convert_fusion.3 = bf16[256,256]{1,0:T(8,128)(2,1)S(1)} fusion(f32[]{:T(128)} %bitcast.32, s32[256]{0:T(256)S(1)} %get-tuple-element.215, f32[]{:T(128)} %bitcast.31, s32[256]{0:T(256)S(1)} %get-tuple-element.216, f32[]{:T(128)} %bitcast.30, s32[256]{0:T(256)S(1)} %get-tuple-element.217, f32[]{:T(128)} %bitcast.29, ...), kind=kOutput, calls=%fused_computation.60 | convolution fusion | flops 208404480 | bytes 161916 | tf_op jit(solution)/shard_map/dot_general | solution.py:48
  44.3 113.9 %while.14 = (s32[]{:T(128)}, bf16[4,8,256,256]{2,3,1,0:T(8,128)(2,1)}, s32[4,8]{1,0:T(4,128)S(1)}, bf16[4,8,256,256]{3,2,1,0:T(8,128)(2,1)}, bf16[256,256]{1,0:T...) while((s32[]{:T(128)}, ...), condition=%wide.region_3.4_spmd.clone.clone, body=%wide.region_2.3_spmd.clone.clone.sunk | while | flops 1084752128 | bytes 28967764 | solution.py:85
  44.4 1.3 dynamic-slice_bitcast_fusion.2
  45.7 0.5 copy.71
  46.2 1.4 bitcast_select_fusion.2
  47.6 1.3 rev.18
  48.9 0.2 broadcast_select_fusion.2
  49.1 11.3 %rev.19 = bf16[8,256,256]{2,1,0:T(8,128)(2,1)} reverse(bf16[8,256,256]{2,1,0:T(8,128)(2,1)S(1)} %broadcast_select_fusion.2), dimensions={2} | reverse | bytes 2097152 | tf_op jit(solution)/shard_map/while/body/eval_jaxpr/rev | solution.py:35
  60.4 2.9 fusion.236
  63.2 1.9 copy.70
  65.2 3.2 fusion.239
  68.3 4.4 %fusion.240 = bf16[4,8,256,256]{2,3,1,0:T(8,128)(2,1)} fusion(bf16[4,8,256,256]{2,3,1,0:T(8,128)(2,1)} %get-tuple-element.303, s32[]{:T(128)} %get-tuple-element.302, bf16[8,256,256]{1,2,0:T(8,128)(2,1)} %fusion.239), kind=kOutput, calls=%fused_computation.7.clone.1 | convolution fusion | flops 540540928 | bytes 2097664 | tf_op jit(solution)/shard_map/while/body/eval_jaxpr/xk,pky->pxy/dot_general | solution.py:76
  72.8 1.3 dynamic-slice_bitcast_fusion.2
  74.1 0.5 copy.71
  74.6 1.4 bitcast_select_fusion.2
  76.0 1.3 rev.18
  77.3 0.2 broadcast_select_fusion.2
  77.5 11.3 %rev.19 = bf16[8,256,256]{2,1,0:T(8,128)(2,1)} reverse(bf16[8,256,256]{2,1,0:T(8,128)(2,1)S(1)} %broadcast_select_fusion.2), dimensions={2} | reverse | bytes 2097152 | tf_op jit(solution)/shard_map/while/body/eval_jaxpr/rev | solution.py:35
  88.8 2.9 fusion.236
  91.7 1.9 copy.70
  93.6 3.2 fusion.239
  96.8 4.5 %fusion.240 = bf16[4,8,256,256]{2,3,1,0:T(8,128)(2,1)} fusion(bf16[4,8,256,256]{2,3,1,0:T(8,128)(2,1)} %get-tuple-element.303, s32[]{:T(128)} %get-tuple-element.302, bf16[8,256,256]{1,2,0:T(8,128)(2,1)} %fusion.239), kind=kOutput, calls=%fused_computation.7.clone.1 | convolution fusion | flops 540540928 | bytes 2097664 | tf_op jit(solution)/shard_map/while/body/eval_jaxpr/xk,pky->pxy/dot_general | solution.py:76
  101.3 1.3 dynamic-slice_bitcast_fusion.2
  102.6 0.5 copy.71
  103.1 1.4 bitcast_select_fusion.2
  104.5 1.3 rev.18
  106.0 11.3 %rev.19 = bf16[8,256,256]{2,1,0:T(8,128)(2,1)} reverse(bf16[8,256,256]{2,1,0:T(8,128)(2,1)S(1)} %broadcast_select_fusion.2), dimensions={2} | reverse | bytes 2097152 | tf_op jit(solution)/shard_map/while/body/eval_jaxpr/rev | solution.py:35
  117.3 2.9 fusion.236
  120.2 1.9 copy.70
  122.1 3.2 fusion.239
  125.3 4.5 %fusion.240 = bf16[4,8,256,256]{2,3,1,0:T(8,128)(2,1)} fusion(bf16[4,8,256,256]{2,3,1,0:T(8,128)(2,1)} %get-tuple-element.303, s32[]{:T(128)} %get-tuple-element.302, bf16[8,256,256]{1,2,0:T(8,128)(2,1)} %fusion.239), kind=kOutput, calls=%fused_computation.7.clone.1 | convolution fusion | flops 540540928 | bytes 2097664 | tf_op jit(solution)/shard_map/while/body/eval_jaxpr/xk,pky->pxy/dot_general | solution.py:76
  129.8 1.3 dynamic-slice_bitcast_fusion.2
  131.1 0.5 copy.71
  131.6 1.4 bitcast_select_fusion.2
  133.0 1.3 rev.18
  134.5 11.3 %rev.19 = bf16[8,256,256]{2,1,0:T(8,128)(2,1)} reverse(bf16[8,256,256]{2,1,0:T(8,128)(2,1)S(1)} %broadcast_select_fusion.2), dimensions={2} | reverse | bytes 2097152 | tf_op jit(solution)/shard_map/while/body/eval_jaxpr/rev | solution.py:35
  145.8 2.9 fusion.236
  148.6 1.9 copy.70
  150.6 3.2 fusion.239
  153.7 4.5 %fusion.240 = bf16[4,8,256,256]{2,3,1,0:T(8,128)(2,1)} fusion(bf16[4,8,256,256]{2,3,1,0:T(8,128)(2,1)} %get-tuple-element.303, s32[]{:T(128)} %get-tuple-element.302, bf16[8,256,256]{1,2,0:T(8,128)(2,1)} %fusion.239), kind=kOutput, calls=%fused_computation.7.clone.1 | convolution fusion | flops 540540928 | bytes 2097664 | tf_op jit(solution)/shard_map/while/body/eval_jaxpr/xk,pky->pxy/dot_general | solution.py:76
  158.2 7.9 %copy.44 = bf16[32,256,256]{2,0,1:T(8,128)(2,1)} copy(bf16[32,256,256]{1,2,0:T(8,128)(2,1)} %bitcast.132) | data formatting | bytes 8388608 | tf_op jit(solution)/shard_map/reshape | solution.py:85
  166.1 7.9 %convolution_convert_fusion.2 = bf16[64,256,256]{2,0,1:T(8,128)(2,1)} fusion(bf16[32,256,256]{2,0,1:T(8,128)(2,1)} %copy.44, s32[32]{0:T(128)S(1)} %multiply_add_fusion.1), kind=kOutput, calls=%fused_computation.55 | convolution fusion | flops 272631808 | bytes 12583040 | tf_op jit(solution)/shard_map/sp,pxy->sxy/dot_general | solution.py:92
  174.0 7.4 %copy.45 = bf16[4,16,256,256]{3,1,2,0:T(8,128)(2,1)} copy(bf16[4,16,256,256]{3,1,0,2:T(8,128)(2,1)} %bitcast.130) | data formatting | bytes 16777216 | tf_op jit(solution)/shard_map/reshape | solution.py:95
  181.4 5.8 %all-to-all-start.1 = ((bf16[4,16,256,256]{3,1,2,0:T(8,128)(2,1)}), bf16[4,16,256,256]{3,1,2,0:T(8,128)(2,1)}, u32[]{:S(2)}, u32[]{:S(2)}) async-start(bf16[4,16,256,256]{3,1,2,0:T(8,128)(2,1)} %copy.45), calls=%async_computation.1 | async-start | bytes 16777216 | tf_op jit(solution)/shard_map/all_to_all | solution.py:102
  187.2 8.8 %all_gather.3 = bf16[6,256,256]{2,1,0:T(8,128)(2,1)S(1)} all-gather(bf16[6,64,256]{2,1,0:T(8,128)(2,1)S(1)} %copy-done), channel_id=1, replica_groups=mesh['groups'=2,'cls'=4,'rep'=4] {'rep'}, dimensions={1}, use_global_device_ids=true | all-gather | bytes 983040 | tf_op jit(solution)/shard_map/all_gather | solution.py:109
  196.0 0.3 fusion.46
  196.4 173.9 %all-to-all-done.1 = bf16[4,16,256,256]{3,1,2,0:T(8,128)(2,1)} async-done(((bf16[4,16,256,256]{3,1,2,0:T(8,128)(2,1)}), bf16[4,16,256,256]{3,1,2,0:T(8,128)(2,1)}, u32[]{:S(2)}, u32[]{:S(2)}) %all-to-all-start.1) | async-done | bytes 8388640 | tf_op jit(solution)/shard_map/all_to_all | solution.py:102
  370.3 13.2 %fusion.48 = f32[4,16]{1,0:T(4,128)S(1)} fusion(bf16[4,16,256,256]{3,1,2,0:T(8,128)(2,1)} %all-to-all-done.1, bf16[6,256,256]{2,1,0:T(8,128)(2,1)S(1)} %all_gather.3, bf16[4,16,6]{1,2,0:T(8,128)(2,1)S(1)} %all-to-all-done), kind=kOutput, calls=%fused_computation.63 | convolution fusion | flops 50332736 | bytes 9176064 | tf_op jit(solution)/shard_map/sjxy,kxy->sjk/dot_general | solution.py:110
  383.5 5.3 %fusion.45 = f32[4,16]{1,0:T(4,128)S(1)} fusion(bf16[4,16,256,256]{3,1,2,0:T(8,128)(2,1)} %all-to-all-done.1), kind=kLoop, calls=%fused_computation.54 | loop fusion | flops 12582848 | bytes 8388864 | tf_op jit(solution)/shard_map/sjxy,sjxy->sj/dot_general | solution.py:106
  388.8 4.7 %convolution_bitcast_fusion = bf16[6,256,256]{2,0,1:T(8,128)(2,1)S(1)} fusion(bf16[4,16,256,256]{3,1,2,0:T(8,128)(2,1)} %all-to-all-done.1, bf16[4,16,6]{1,2,0:T(8,128)(2,1)S(1)} %all-to-all-done, bf16[4,16]{1,0:T(4,128)(2,1)S(1)} %get-tuple-element.179), kind=kOutput, calls=%fused_computation.56 | convolution fusion | flops 50333184 | bytes 9175936 | tf_op jit(solution)/shard_map/sjk,sjxy->kxy/dot_general | solution.py:120
  393.4 1.1 copy.67
  394.6 5.8 %psum.15 = bf16[6]{0:T(256)(128)(2,1)S(1)} all-reduce(bf16[6]{0:T(256)(128)(2,1)S(1)} %fusion.191), channel_id=1, replica_groups=mesh['groups'=2,'cls'=4,'rep'=4] {'rep'}, use_global_device_ids=true, to_apply=%region_8.9 | all-reduce | flops 6 | bytes 24 | tf_op jit(solution)/shard_map/psum | solution.py:125
  400.4 28.0 %all-reduce.2.cloned.1.call-done = bf16[6,256,256]{2,1,0:T(8,128)(2,1)} async-done(((bf16[6,256,256]{2,1,0:T(8,128)(2,1)}), bf16[6,256,256]{2,1,0:T(8,128)(2,1)}) %all-reduce.2.cloned.1.call-update) | async-done | bytes 786448 | tf_op jit(solution)/shard_map/psum | solution.py:124
  428.4 1.8 add_divide_fusion
  (43 shorter events, 1.1 us)
Async XLA Ops:
  8.5 172.9 %all-to-all-start = ((bf16[4,16,6]{1,2,0:T(8,128)(2,1)}), bf16[4,16,6]{1,2,0:T(8,128)(2,1)S(1)}, u32[]{:S(2)}, u32[]{:S(2)}) async-start(bf16[4,16,6]{1,2,0:T(8,128)(2,1)} %copy.42), calls=%async_computation | async-start | bytes 16384 | tf_op jit(solution)/shard_map/all_to_all | solution.py:103
  181.4 5.8 %copy-start = (bf16[6,64,256]{2,1,0:T(8,128)(2,1)S(1)}, bf16[6,64,256]{2,1,0:T(8,128)(2,1)}, u32[]{:S(2)}) copy-start(bf16[6,64,256]{2,1,0:T(8,128)(2,1)} %param.15) | copy-start | bytes 589828
  181.4 188.9 %all-to-all-start.1 = ((bf16[4,16,256,256]{3,1,2,0:T(8,128)(2,1)}), bf16[4,16,256,256]{3,1,2,0:T(8,128)(2,1)}, u32[]{:S(2)}, u32[]{:S(2)}) async-start(bf16[4,16,256,256]{3,1,2,0:T(8,128)(2,1)} %copy.45), calls=%async_computation.1 | async-start | bytes 16777216 | tf_op jit(solution)/shard_map/all_to_all | solution.py:102
  187.2 241.2 %all-reduce.2.cloned.1.call-start = ((), (), s32[]{:S(2)}) async-start(), calls=%async_computation.2 | async-start | bytes 1572864 | tf_op jit(solution)/shard_map/psum | solution.py:124
Sparse Core Ops, SparseCore 0:
  394.6 33.7 all-reduce.1
where the time goes:
time: 439 us; the launch traced here: 437 us
  waiting for transfers between devices  202 us (46%)
  local copies, waits for them, and re-layouts  89.9 us (20%)
  matrix products  89.8 us (20%)
  other arithmetic  15 us (3%)
  blocking collectives  14.6 us (3%)
  between operations  13.6 us (3%)
  starting transfers between devices  12.1 us (3%)
    all_to_all x1, waiting for transfers between devices, local(): lax.all_to_all(outgoing, 'cls', split_axis=0, concat_axis=0, tiled=True)  174 us
    rev x4, local copies, waits for them, and re-layouts, orient(): return jnp.where(flip_cols, turned[:, :, ::-1], turned)  45.1 us
    psum x1, waiting for transfers between devices, local(): lax.psum(class_sums.astype(jnp.bfloat16), 'rep').astype(jnp.float32)  28 us
    dot_general x1, matrix products, local(): jnp.dot(hartley, band_table(filter_taps, tile_len), preferred_element_typ...  21.8 us
    dot_general x4, matrix products, filter_group(): jnp.einsum('xk,pky->pxy', synthesis, second_pass, preferred_element_type=...  17.9 us
    dot_general x1, matrix products, local(): jnp.einsum('sjxy,kxy->sjk', arrived, piece, preferred_element_type=jnp.fl...  13.2 us
    dot_general x4, matrix products, filter_group(): jnp.einsum('li,pim->plm', analysis, first_pass, preferred_element_type=jn...  12.6 us
    dot_general x4, matrix products, filter_group(): jnp.einsum('pb,bxy->pxy', bin_hits, ctf_table, preferred_element_type=jnp...  11.5 us
  transfers between devices with their start and end apart: 3, of which 2 were waited for; matrix products, arithmetic and copies ran while one was open for 38% of the time, Pallas kernels for 0%

commit v1 on v0

v1 whole, which is shorter than its diff:
```python
import functools
import math

import numpy as np

import jax
import jax.numpy as jnp
from jax import lax
from jax.experimental import pallas as pl
from jax.experimental.pallas import tpu as pltpu
from jax.sharding import PartitionSpec as P

EPSILON = 1e-05
PRIOR_WEIGHT = 4.0
F32 = jnp.float32
BF16 = jnp.bfloat16
MIB = 1 << 20


def hartley_table(tile_len):
    index = np.arange(tile_len, dtype=np.int64)
    phases = 2.0 * np.pi / tile_len * (index[:, None] * index[None, :] % tile_len)
    return (np.cos(phases) + np.sin(phases)).astype(np.float32)


def filter_kernel(
    turn_ref, bin_ref, taps_ref, hartley_ref, ctf_ref, tile_ref, out_ref, fwd, fwd_t, syn
):
    batch, tile_len, _ = tile_ref.shape
    taps = taps_ref.shape[0]
    half = (taps - 1) // 2
    step = pl.program_id(0)

    @pl.when(step == 0)
    def _():
        row = lax.broadcasted_iota(jnp.int32, (tile_len, tile_len), 0)
        col = lax.broadcasted_iota(jnp.int32, (tile_len, tile_len), 1)
        gap = col - row
        band = jnp.zeros((tile_len, tile_len), F32)
        for tap in range(taps):
            band = jnp.where(gap == tap - half, taps_ref[tap], band)
        hartley = hartley_ref[...]
        analysis = jnp.dot(
            hartley, band, preferred_element_type=F32, precision=lax.Precision.HIGHEST
        ).astype(BF16)
        mirror = jnp.where(row + col == tile_len - 1, 1.0, 0.0).astype(BF16)
        mirrored = jnp.dot(analysis, mirror, preferred_element_type=F32)
        fwd[0] = analysis
        fwd[1] = mirrored.astype(BF16)
        fwd_t[0] = analysis.astype(F32).T.astype(BF16)
        fwd_t[1] = mirrored.T.astype(BF16)
        syn[...] = hartley.astype(BF16)

    for i in range(batch):
        code = turn_ref[step * batch + i]
        tile = tile_ref[i]
        tile = jnp.where(code >= 4, tile.T, tile)
        first = jnp.dot(tile, fwd_t[(code // 2) % 2], preferred_element_type=F32).astype(BF16)
        raw = jnp.dot(fwd[code % 2], first, preferred_element_type=F32)
        gain = ctf_ref[bin_ref[step * batch + i]].astype(F32)
        spectra = (raw * gain).astype(BF16)
        second = jnp.dot(spectra, syn[...], preferred_element_type=F32).astype(BF16)
        result = jnp.dot(syn[...], second, preferred_element_type=F32)
        out_ref[i] = (result * (1.0 / (tile_len * tile_len))).astype(BF16)


def filter_tiles(particles, rotation, defocus, filter_taps, ctf_table):
    count, tile_len, _ = particles.shape
    batch = math.gcd(count, 4)
    hartley = jnp.asarray(hartley_table(tile_len))
    square = (tile_len, tile_len)
    grid_spec = pltpu.PrefetchScalarGridSpec(
        num_scalar_prefetch=3,
        grid=(count // batch,),
        in_specs=[
            pl.BlockSpec(square, lambda i, *_: (0, 0)),
            pl.BlockSpec(ctf_table.shape, lambda i, *_: (0, 0, 0)),
            pl.BlockSpec((batch,) + square, lambda i, *_: (i, 0, 0)),
        ],
        out_specs=pl.BlockSpec((batch,) + square, lambda i, *_: (i, 0, 0)),
        scratch_shapes=[
            pltpu.VMEM((2,) + square, BF16),
            pltpu.VMEM((2,) + square, BF16),
            pltpu.VMEM(square, BF16),
        ],
    )
    return pl.pallas_call(
        filter_kernel,
        grid_spec=grid_spec,
        out_shape=jax.ShapeDtypeStruct(particles.shape, BF16),
        compiler_params=pltpu.CompilerParams(vmem_limit_bytes=24 * MIB),
        cost_estimate=pl.CostEstimate(
            flops=8 * count * tile_len**3,
            bytes_accessed=4 * count * tile_len**2,
            transcendentals=0,
        ),
        name="filter_tiles",
    )(rotation, defocus, filter_taps, hartley, ctf_table, particles)


def weigh_kernel(class_ref, tile_ref, refs_ref, sum_ref, weight_ref, acc, start, order):
    count, tile_len, _ = tile_ref.shape
    _, reps, own, rows, _ = refs_ref.shape
    owners = pl.num_programs(0)
    owner = pl.program_id(0)
    scale = 1.0 / (tile_len * tile_len)

    @pl.when(owner == 0)
    def _():
        def clear(i, carry):
            start[i] = 0
            return carry

        lax.fori_loop(0, owners + 1, clear, 0)

        def tally(i, carry):
            slot = class_ref[i] // own + 1
            start[slot] = start[slot] + 1
            return carry

        lax.fori_loop(0, count, tally, 0)

        def running(i, carry):
            total = carry + start[i]
            start[i] = total
            return total

        lax.fori_loop(0, owners + 1, running, 0)

        def place(i, carry):
            slot = class_ref[i] // own
            where = start[slot]
            order[where] = i
            start[slot] = where + 1
            return carry

        lax.fori_loop(0, count, place, 0)

    end = start[owner]
    begin = jnp.where(owner == 0, 0, start[jnp.maximum(owner - 1, 0)])
    acc[...] = jnp.zeros_like(acc)
    weight_ref[...] = jnp.zeros_like(weight_ref)
    row = lax.broadcasted_iota(jnp.int32, weight_ref.shape[1:], 0)

    def total(values):
        return jnp.sum(jnp.sum(values, axis=0, keepdims=True), axis=1, keepdims=True)

    def body(i, carry):
        p = order[i]
        k = class_ref[p] - owner * own
        tile = tile_ref[p].astype(F32)
        image = refs_ref[0, :, k].reshape(tile_len, tile_len).astype(F32)
        power = total(tile * tile) * scale
        ref_power = total(image * image) * scale
        meet = total(tile * image) * scale
        score = meet / jnp.sqrt((power + EPSILON) * (ref_power + EPSILON))
        weight = 1.0 / (1.0 + jnp.exp(-tile_len * score))
        scaling = (weight / jnp.sqrt(power + EPSILON)).astype(BF16).astype(F32)
        acc[k] += scaling * tile
        weight_ref[0] += jnp.where(row == k, weight, 0.0)
        return carry

    lax.fori_loop(begin, end, body, 0)
    for k in range(own):
        sum_ref[0, :, k] = acc[k].astype(BF16).reshape(reps, rows, tile_len)


def weigh(filtered, classes, refs):
    count, tile_len, _ = filtered.shape
    owners, reps, own, rows, _ = refs.shape
    slots = -(-own // 8) * 8
    block = (1, reps, own, rows, tile_len)
    grid_spec = pltpu.PrefetchScalarGridSpec(
        num_scalar_prefetch=1,
        grid=(owners,),
        in_specs=[
            pl.BlockSpec(filtered.shape, lambda o, *_: (0, 0, 0)),
            pl.BlockSpec(block, lambda o, *_: (o, 0, 0, 0, 0)),
        ],
        out_specs=[
            pl.BlockSpec(block, lambda o, *_: (o, 0, 0, 0, 0)),
            pl.BlockSpec((1, slots, 128), lambda o, *_: (o, 0, 0)),
        ],
        scratch_shapes=[
            pltpu.VMEM((own, tile_len, tile_len), F32),
            pltpu.SMEM((owners + 1,), jnp.int32),
            pltpu.SMEM((count,), jnp.int32),
        ],
    )
    return pl.pallas_call(
        weigh_kernel,
        grid_spec=grid_spec,
        out_shape=[
            jax.ShapeDtypeStruct(refs.shape, BF16),
            jax.ShapeDtypeStruct((owners, slots, 128), F32),
        ],
        compiler_params=pltpu.CompilerParams(vmem_limit_bytes=32 * MIB),
        name="weigh_tiles",
    )(classes, filtered, refs)


def local(particles, classes, rotation, defocus, filter_taps, ctf_table, references):
    owners = lax.axis_size("cls")
    reps = lax.axis_size("rep")
    own, rows, tile_len = references.shape
    refs = lax.all_gather(references, ("cls", "rep"), axis=0, tiled=False)
    refs = refs.reshape(owners, reps, own, rows, tile_len)
    filtered = filter_tiles(particles, rotation, defocus, filter_taps, ctf_table)
    sums, weights = weigh(filtered, classes, refs)
    sums = lax.psum_scatter(sums, "rep", scatter_dimension=1, tiled=False)
    sums = lax.psum_scatter(sums, "cls", scatter_dimension=0, tiled=False)
    weights = lax.psum(weights[:, :own, 0], ("cls", "rep"))
    total = lax.dynamic_index_in_dim(weights, lax.axis_index("cls"), 0, keepdims=False)
    return (PRIOR_WEIGHT * references.astype(F32) + sums.astype(F32)) / (
        PRIOR_WEIGHT + total[:, None, None]
    )


def solution(mesh):
    placed = (
        P(("groups", "cls", "rep"), None, None),
        P(("groups", "cls", "rep")),
        P(("groups", "cls", "rep")),
        P(("groups", "cls", "rep")),
        P(),
        P(),
        P(("groups", "cls"), "rep", None),
    )
    return jax.shard_map(
        local,
        mesh=mesh,
        in_specs=placed,
        out_specs=P(("groups", "cls"), "rep", None),
        check_vma=False,
    )
```

time: 439 us -> 184 us (0.42)
  waiting for transfers between devices: 202 us -> 93.1 us
  matrix products: 89.8 us -> 0 us
  local copies, waits for them, and re-layouts: 89.9 us -> 16.2 us
  Pallas kernels: 0 us -> 26.3 us
  blocking collectives: 14.6 us -> 33 us
  other arithmetic: 15 us -> 1.79 us
  starting transfers between devices: 12.1 us -> 0.08 us
    all_to_all x2 -> x0, waiting for transfers between devices: 174 us -> none  [the longest x1 174 us: local(): lax.all_to_all(outgoing, 'cls', split_axis=0, concat_axis=0, tiled=True)]
    dot_general x17 -> x0, matrix products: 89.8 us -> none  [the longest x1 21.8 us: local(): jnp.dot(hartley, band_table(filter_taps, tile_len), preferred_element_typ...]
    unnamed x1 -> x4, waiting for transfers between devices: 0.02 us -> 66.9 us
    rev x8 -> x0, local copies, waits for them, and re-layouts: 50.2 us -> none  [the longest x4 45.1 us: orient(): return jnp.where(flip_cols, turned[:, :, ::-1], turned)]
    psum x1 -> x0, waiting for transfers between devices: 28 us -> none  [local(): lax.psum(class_sums.astype(jnp.bfloat16), 'rep').astype(jnp.float32)]
    psum x1, blocking collectives: 5.79 us -> 33 us  [local(): weights = lax.psum(weights[:, :own, 0], ('cls', 'rep'))]
    pallas_call x0 -> x2, Pallas kernels: none -> 26.3 us  [the longest x1 16.3 us: filter_tiles(): pl.pallas_call(filter_kernel, grid_spec=grid_spec, out_shape=jax.ShapeDty...]
    all_gather x0 -> x1, waiting for transfers between devices: none -> 26.1 us  [local(): refs = lax.all_gather(references, ('cls', 'rep'), axis=0, tiled=False)]
  transfers between devices with their start and end apart: 3 -> 3, of which waited for: 2 -> 2; matrix products, arithmetic and copies ran while one was open for 38% -> 0% of each run, Pallas kernels for 0% -> 9%
where the time goes in v1:
time: 184 us
  waiting for transfers between devices  93.1 us (51%)
  blocking collectives  33 us (18%)
  Pallas kernels  26.3 us (14%)
  local copies, waits for them, and re-layouts  16.2 us (9%)
  between operations  13.2 us (7%)
    unnamed x4, waiting for transfers between devices  66.9 us
    psum x1, blocking collectives, local(): weights = lax.psum(weights[:, :own, 0], ('cls', 'rep'))  33 us
    all_gather x1, waiting for transfers between devices, local(): refs = lax.all_gather(references, ('cls', 'rep'), axis=0, tiled=False)  26.1 us
    pallas_call x1, Pallas kernels, filter_tiles(): pl.pallas_call(filter_kernel, grid_spec=grid_spec, out_shape=jax.ShapeDty...  16.3 us
    unnamed x25, local copies, waits for them, and re-layouts  13.3 us
    pallas_call x1, Pallas kernels, weigh(): pl.pallas_call(weigh_kernel, grid_spec=grid_spec, out_shape=[jax.ShapeDty...  10.1 us
  transfers between devices with their start and end apart: 3, of which 2 were waited for; matrix products, arithmetic and copies ran while one was open for 0% of the time, Pallas kernels for 9%

profile of v1, /device:TPU:0, one launch (start us, length us, event | category | flops | bytes accessed | tf_op | source)
XLA Modules:
  0.0 183.6 jit_solution(13757810440912647899)
XLA Ops:
  6.5 0.0 all-gather.3.cloned.1.call-start
  6.5 0.7 all-gather.3.cloned.1.call-update
  7.3 0.0 copy-start.3
  7.3 0.0 all-reduce.3.cloned.1.call-start
  7.3 0.0 copy-start.4
  7.3 2.2 %copy-done.4 = bf16[32,256,256]{2,1,0:T(8,128)(2,1)S(1)} copy-done((bf16[32,256,256]{2,1,0:T(8,128)(2,1)S(1)}, bf16[32,256,256]{2,1,0:T(8,128)(2,1)}, u32[]{:S(2)}) %copy-start.4) | copy-done | bytes 4194328
  9.5 0.0 copy-start.5
  9.5 1.0 copy-done.5
  10.5 0.0 copy-start.6
  10.5 0.7 copy-done.6
  11.2 0.0 copy-start.7
  11.2 0.7 copy-done.7
  11.9 0.0 copy-start.8
  11.9 0.7 copy-done.8
  12.5 0.0 copy-start.9
  12.5 0.9 copy-done.9
  13.5 16.3 %filter_tiles.1.tile_ref = bf16[32,256,256]{2,1,0:T(8,128)(2,1)S(1)} custom-call(s32[32]{0:T(128)S(1)} %copy-done.6, s32[32]{0:T(128)S(1)} %copy-done.7, f32[31]{0:T(128)S(1)} %copy-done.8, f32[256,256]{1,0:T(8,128)S(1)} %copy-done.9, bf16[4,256,256]{2,1,0:T(8,128)(2,1)S(1)} %copy-done.5, bf16[32,256,256]{2,1,0:T(8,128)(2,1)S(1)} %copy-done.4), custom_call_target="tpu_custom_call" | custom-call | flops 4294967296 | bytes 8388608 | tf_op jit(solution)/shard_map/filter_tiles/pallas_call | solution.py:87
  29.7 0.0 copy-start
  29.7 1.9 %copy-done = bf16[32,256,256]{2,1,0:T(8,128)(2,1)} copy-done((bf16[32,256,256]{2,1,0:T(8,128)(2,1)}, bf16[32,256,256]{2,1,0:T(8,128)(2,1)S(1)}, u32[]{:S(2)}) %copy-start) | copy-done | bytes 4194328
  31.7 26.1 %all-gather.3.cloned.1.call-done = bf16[96,64,256]{2,1,0:T(8,128)(2,1)} async-done(((bf16[6,64,256]{2,1,0:T(8,128)(2,1)}), bf16[96,64,256]{2,1,0:T(8,128)(2,1)}) %all-gather.3.cloned.1.call-update) | async-done | bytes 3145744 | tf_op jit(solution)/shard_map/all_gather | solution.py:206
  57.8 0.0 copy-done.3
  57.8 0.0 copy-start.1
  57.8 2.2 %copy-done.1 = bf16[32,256,256]{2,1,0:T(8,128)(2,1)S(1)} copy-done((bf16[32,256,256]{2,1,0:T(8,128)(2,1)S(1)}, bf16[32,256,256]{2,1,0:T(8,128)(2,1)}, u32[]{:S(2)}) %copy-start.1) | copy-done | bytes 4194328
  60.0 0.0 copy-start.2
  60.0 1.9 %copy-done.2 = bf16[96,64,256]{2,1,0:T(8,128)(2,1)S(1)} copy-done((bf16[96,64,256]{2,1,0:T(8,128)(2,1)S(1)}, bf16[96,64,256]{2,1,0:T(8,128)(2,1)}, u32[]{:S(2)}) %copy-start.2) | copy-done | bytes 3145752
  61.9 10.1 %weigh_tiles.1 = (bf16[4,4,6,64,256]{4,3,2,1,0:T(8,128)(2,1)}, f32[4,8,128]{2,1,0:T(8,128)S(1)}) custom-call(s32[32]{0:T(128)S(1)} %copy-done.3, bf16[32,256,256]{2,1,0:T(8,128)(2,1)S(1)} %copy-done.1, bf16[4,4,6,64,256]{4,3,2,1,0:T(8,128)(2,1)S(1)} %bitcast.15), custom_call_target="tpu_custom_call" | custom-call | tf_op jit(solution)/shard_map/weigh_tiles/pallas_call | solution.py:190
  71.9 0.0 copy-start.11
  71.9 0.0 copy-start.10
  71.9 0.0 all-reduce.3.cloned.1.call-update
  72.0 0.0 reduce-scatter.5.cloned.1.call-start
  72.0 0.6 copy-done.11
  72.6 0.6 dynamic-slice
  73.2 66.2 %all-reduce.3.cloned.1.call-done = bf16[4,4,6,64,256]{4,3,2,1,0:T(8,128)(2,1)} async-done(((bf16[4,4,6,64,256]{4,3,2,1,0:T(8,128)(2,1)}), bf16[4,4,6,64,256]{4,3,2,1,0:T(8,128)(2,1)}) %all-reduce.3.cloned.1.call-update) | async-done | bytes 3145744
  139.4 2.7 %dynamic-slice_bitcast_fusion = bf16[4,6,64,256]{3,2,1,0:T(8,128)(2,1)} fusion(bf16[4,4,6,64,256]{4,3,2,1,0:T(8,128)(2,1)} %all-reduce.3.cloned.1.call-done, u32[]{:T(128)} %bitcast.7), kind=kLoop, calls=%fused_computation | loop fusion | bytes 1572868 | tf_op jit(solution)/shard_map/reduce_scatter | solution.py:210
  142.1 0.0 reduce-scatter.5.cloned.1.call-update
  142.1 0.1 slice_reduce_fusion
  142.2 33.0 %psum.7 = f32[4,6]{1,0:T(4,128)S(1)} all-reduce(f32[4,6]{1,0:T(4,128)S(1)} %slice_reduce_fusion), channel_id=1, replica_groups=mesh['groups'=2,'cls'=4,'rep'=4] {'cls','rep'}, use_global_device_ids=true, to_apply=%region_2.0 | all-reduce | flops 24 | bytes 192 | tf_op jit(solution)/shard_map/psum | solution.py:212
  175.2 0.0 reduce-scatter.5.cloned.1.call-done
  175.3 0.0 copy-done.10
  175.3 1.8 fusion
  (1 shorter events, 0.0 us)
Async XLA Ops:
  6.5 51.3 %all-gather.3.cloned.1.call-start = ((), (), s32[]{:S(2)}) async-start(), calls=%async_computation.2 | async-start | bytes 3342336 | tf_op jit(solution)/shard_map/all_gather | solution.py:206
  7.3 50.6 %copy-start.3 = (s32[32]{0:T(128)S(1)}, s32[32]{0:T(128)}, u32[]{:S(2)}) copy-start(s32[32]{0:T(128)} %class_ref.1) | copy-start | bytes 388
  7.3 132.1 %all-reduce.3.cloned.1.call-start = ((), (), s32[]{:S(2)}) async-start(), calls=%async_computation.3 | async-start | bytes 6291456
  7.3 2.2 %copy-start.4 = (bf16[32,256,256]{2,1,0:T(8,128)(2,1)S(1)}, bf16[32,256,256]{2,1,0:T(8,128)(2,1)}, u32[]{:S(2)}) copy-start(bf16[32,256,256]{2,1,0:T(8,128)(2,1)} %tile_ref.1) | copy-start | bytes 12582916
  9.5 1.0 copy-start.5
  10.5 0.7 copy-start.6
  11.2 0.7 copy-start.7
  11.9 0.7 copy-start.8
  12.5 0.9 copy-start.9
  29.7 1.9 %copy-start = (bf16[32,256,256]{2,1,0:T(8,128)(2,1)}, bf16[32,256,256]{2,1,0:T(8,128)(2,1)S(1)}, u32[]{:S(2)}) copy-start(bf16[32,256,256]{2,1,0:T(8,128)(2,1)S(1)} %filter_tiles.1.tile_ref) | copy-start | bytes 12582916
  57.8 2.2 %copy-start.1 = (bf16[32,256,256]{2,1,0:T(8,128)(2,1)S(1)}, bf16[32,256,256]{2,1,0:T(8,128)(2,1)}, u32[]{:S(2)}) copy-start(bf16[32,256,256]{2,1,0:T(8,128)(2,1)} %copy-done) | copy-start | bytes 12582916
  60.0 1.9 %copy-start.2 = (bf16[96,64,256]{2,1,0:T(8,128)(2,1)S(1)}, bf16[96,64,256]{2,1,0:T(8,128)(2,1)}, u32[]{:S(2)}) copy-start(bf16[96,64,256]{2,1,0:T(8,128)(2,1)} %all-gather.3.cloned.1.call-done) | copy-start | bytes 9437188
  71.9 0.7 copy-start.11
  71.9 103.3 %copy-start.10 = (bf16[6,64,256]{2,1,0:T(8,128)(2,1)S(1)}, bf16[6,64,256]{2,1,0:T(8,128)(2,1)}, u32[]{:S(2)}) copy-start(bf16[6,64,256]{2,1,0:T(8,128)(2,1)} %param.14) | copy-start | bytes 589828
  72.0 103.3 %reduce-scatter.5.cloned.1.call-start = ((), (), s32[]{:S(2)}) async-start(), calls=%async_computation.1 | async-start | bytes 983040 | tf_op jit(solution)/shard_map/reduce_scatter | solution.py:211
Sparse Core Ops, SparseCore 0:
  9.6 48.1 all-gather.2
  72.1 67.2 all-reduce.2
  142.3 23.5 reduce-scatter.4

commit v2 on v1

--- a/solution.py
+++ b/solution.py
@@ -101,6 +101,7 @@
 def weigh_kernel(class_ref, tile_ref, refs_ref, sum_ref, weight_ref, acc, start, order):
     count, tile_len, _ = tile_ref.shape
     _, reps, own, rows, _ = refs_ref.shape
+    lanes = sum_ref.shape[1]
     owners = pl.num_programs(0)
     owner = pl.program_id(0)
     scale = 1.0 / (tile_len * tile_len)
@@ -162,14 +163,17 @@
 
     lax.fori_loop(begin, end, body, 0)
     for k in range(own):
-        sum_ref[0, :, k] = acc[k].astype(BF16).reshape(reps, rows, tile_len)
-
-
-def weigh(filtered, classes, refs):
+        whole = acc[k].astype(BF16).reshape(reps, rows, tile_len)
+        for rep in range(reps):
+            sum_ref[0, rep % lanes, rep // lanes, k] = whole[rep]
+
+
+def weigh(filtered, classes, refs, lanes):
     count, tile_len, _ = filtered.shape
     owners, reps, own, rows, _ = refs.shape
     slots = -(-own // 8) * 8
     block = (1, reps, own, rows, tile_len)
+    parted = (owners, lanes, reps // lanes, own, rows, tile_len)
     grid_spec = pltpu.PrefetchScalarGridSpec(
         num_scalar_prefetch=1,
         grid=(owners,),
@@ -178,7 +182,7 @@
             pl.BlockSpec(block, lambda o, *_: (o, 0, 0, 0, 0)),
         ],
         out_specs=[
-            pl.BlockSpec(block, lambda o, *_: (o, 0, 0, 0, 0)),
+            pl.BlockSpec((1,) + parted[1:], lambda o, *_: (o, 0, 0, 0, 0, 0)),
             pl.BlockSpec((1, slots, 128), lambda o, *_: (o, 0, 0)),
         ],
         scratch_shapes=[
@@ -191,12 +195,139 @@
         weigh_kernel,
         grid_spec=grid_spec,
         out_shape=[
-            jax.ShapeDtypeStruct(refs.shape, BF16),
+            jax.ShapeDtypeStruct(parted, BF16),
             jax.ShapeDtypeStruct((owners, slots, 128), F32),
         ],
         compiler_params=pltpu.CompilerParams(vmem_limit_bytes=32 * MIB),
         name="weigh_tiles",
     )(classes, filtered, refs)
+
+
+def reduce_kernel(
+    sum_ref, weight_ref, own_ref, out_ref, near, far, share, deep, w_near, w_far, w_share, w_deep,
+    near_sem, far_send, far_recv, deep_send, deep_recv, wn_sem, wf_send, wf_recv, wd_send, wd_recv
+):
+    owners, lanes, chips, own, rows, _ = sum_ref.shape
+    me_z = lax.axis_index("cls")
+    rep = lax.axis_index("rep")
+    me_x, lane = rep // lanes, rep % lanes
+    twin = {"rep": me_x * lanes + (1 - lane)}
+    peers_x = [(me_x + d) % chips for d in range(1, chips)]
+    peers_z = [(me_z + d) % owners for d in range(1, owners)]
+
+    def copy(src, dst, send, recv, device):
+        return pltpu.make_async_remote_copy(
+            src_ref=src,
+            dst_ref=dst,
+            send_sem=send,
+            recv_sem=recv,
+            device_id=device,
+            device_id_type=pl.DeviceIdType.MESH,
+        )
+
+    def to_x(x):
+        return {"rep": x * lanes + lane}
+
+    barrier = pltpu.get_barrier_semaphore()
+    for device in [twin] + [to_x(x) for x in peers_x] + [{"cls": z} for z in peers_z]:
+        pl.semaphore_signal(
+            barrier, inc=1, device_id=device, device_id_type=pl.DeviceIdType.MESH
+        )
+    pl.semaphore_wait(barrier, chips + owners - 1)
+
+    sends = []
+
+    def launch(made):
+        made.start()
+        sends.append(made)
+
+    order = peers_z + [me_z]
+    launch(copy(weight_ref, w_near, wn_sem.at[0], wn_sem.at[1], twin))
+    for o in order:
+        launch(copy(sum_ref.at[o, 1 - lane], near.at[o], near_sem.at[0, o], near_sem.at[1, o], twin))
+
+    copy(weight_ref, w_near, wn_sem.at[0], wn_sem.at[1], twin).wait_recv()
+    w_share[...] = weight_ref[...] + w_near[...]
+    for x in peers_x:
+        launch(copy(w_share, w_far.at[me_x], wf_send.at[x], wf_recv.at[me_x], to_x(x)))
+    for o in order:
+        copy(
+            sum_ref.at[o, lane], near.at[o], near_sem.at[0, o], near_sem.at[1, o], twin
+        ).wait_recv()
+        near[o] = (near[o].astype(F32) + sum_ref[o, lane].astype(F32)).astype(BF16)
+        for x in peers_x:
+            launch(
+                copy(near.at[o, x], far.at[me_x, o], far_send.at[x, o], far_recv.at[me_x, o], to_x(x))
+            )
+    w_total = w_share[...]
+    for x in peers_x:
+        copy(w_share, w_far.at[x], wf_send.at[x], wf_recv.at[x], to_x(x)).wait_recv()
+        w_total = w_total + w_far[x]
+    for x in peers_x:
+        made = copy(w_share, w_far.at[me_x], wf_send.at[x], wf_recv.at[me_x], to_x(x))
+        made.wait_send()
+        sends.pop(1 + owners)
+    w_share[...] = w_total
+    for z in peers_z:
+        launch(copy(w_share.at[z], w_deep.at[me_z], wd_send.at[z], wd_recv.at[me_z], {"cls": z}))
+    for o in order:
+        total = near[o, me_x].astype(F32)
+        for x in peers_x:
+            copy(near.at[o, x], far.at[x, o], far_send.at[x, o], far_recv.at[x, o], to_x(x)).wait_recv()
+            total = total + far[x, o].astype(F32)
+        share[o] = total.astype(BF16)
+        if o is not me_z:
+            launch(copy(share.at[o], deep.at[me_z], deep_send.at[o], deep_recv.at[me_z], {"cls": o}))
+    w_mine = w_share[me_z]
+    for z in peers_z:
+        copy(w_share.at[z], w_deep.at[z], wd_send.at[z], wd_recv.at[z], {"cls": z}).wait_recv()
+        w_mine = w_mine + w_deep[z]
+    for z in peers_z:
+        copy(share.at[z], deep.at[z], deep_send.at[z], deep_recv.at[z], {"cls": z}).wait_recv()
+    for k in range(own):
+        total = PRIOR_WEIGHT * own_ref[k].astype(F32) + share[me_z, k].astype(F32)
+        for z in peers_z:
+            total = total + deep[z, k].astype(F32)
+        out_ref[k] = total / (PRIOR_WEIGHT + w_mine[k : k + 1, 0:1])
+    for made in sends:
+        made.wait_send()
+
+
+def reduce_update(sums, weights, references):
+    owners, lanes, chips, own, rows, tile_len = sums.shape
+    slots = weights.shape[1:]
+    piece = (own, rows, tile_len)
+    dma = pltpu.SemaphoreType.DMA
+    return pl.pallas_call(
+        reduce_kernel,
+        out_shape=jax.ShapeDtypeStruct(references.shape, F32),
+        in_specs=[pl.BlockSpec(memory_space=pltpu.VMEM)] * 3,
+        out_specs=pl.BlockSpec(memory_space=pltpu.VMEM),
+        scratch_shapes=[
+            pltpu.VMEM((owners, chips) + piece, BF16),
+            pltpu.VMEM((chips, owners) + piece, BF16),
+            pltpu.VMEM((owners,) + piece, BF16),
+            pltpu.VMEM((owners,) + piece, BF16),
+            pltpu.VMEM((owners,) + slots, F32),
+            pltpu.VMEM((chips, owners) + slots, F32),
+            pltpu.VMEM((owners,) + slots, F32),
+            pltpu.VMEM((owners,) + slots, F32),
+            dma((2, owners)),
+            dma((chips, owners)),
+            dma((chips, owners)),
+            dma((owners,)),
+            dma((owners,)),
+            dma((2,)),
+            dma((chips,)),
+            dma((chips,)),
+            dma((owners,)),
+            dma((owners,)),
+        ],
+        compiler_params=pltpu.CompilerParams(
+            collective_id=1, has_side_effects=True, vmem_limit_bytes=32 * MIB
+        ),
+        name="reduce_update",
+    )(sums, weights, references)
 
 
 def local(particles, classes, rotation, defocus, filter_taps, ctf_table, references):
@@ -206,7 +337,11 @@
     refs = lax.all_gather(references, ("cls", "rep"), axis=0, tiled=False)
     refs = refs.reshape(owners, reps, own, rows, tile_len)
     filtered = filter_tiles(particles, rotation, defocus, filter_taps, ctf_table)
-    sums, weights = weigh(filtered, classes, refs)
+    small = reps % 2 == 0 and refs.size <= 4 * MIB
+    sums, weights = weigh(filtered, classes, refs, 2 if small else 1)
+    if small:
+        return reduce_update(sums, weights, references)
+    sums = sums.reshape(refs.shape)
     sums = lax.psum_scatter(sums, "rep", scatter_dimension=1, tiled=False)
     sums = lax.psum_scatter(sums, "cls", scatter_dimension=0, tiled=False)
     weights = lax.psum(weights[:, :own, 0], ("cls", "rep"))

time: 184 us -> 107 us (0.58)
  waiting for transfers between devices: 93.1 us -> 26.9 us
  blocking collectives: 33 us -> 0 us
  Pallas kernels: 26.3 us -> 53.9 us
  local copies, waits for them, and re-layouts: 16.2 us -> 12.9 us
    unnamed x4 -> x1, waiting for transfers between devices: 66.9 us -> 0.71 us
    psum x1 -> x0, blocking collectives: 33 us -> none  [local(): weights = lax.psum(weights[:, :own, 0], ('cls', 'rep'))]
    pallas_call x0 -> x1, Pallas kernels: none -> 29.1 us  [reduce_update(): pl.pallas_call(reduce_kernel, out_shape=jax.ShapeDtypeStruct(references.s...]
    reduce_scatter x1 -> x0, local copies, waits for them, and re-layouts: 2.75 us -> none  [local(): sums = lax.psum_scatter(sums, 'rep', scatter_dimension=1, tiled=False)]
    unnamed x25 -> x23, local copies, waits for them, and re-layouts: 13.3 us -> 12.9 us
  transfers between devices with their start and end apart: 3 -> 1, of which waited for: 2 -> 1; matrix products, arithmetic and copies ran while one was open for 0% -> 0% of each run, Pallas kernels for 9% -> 15%
where the time goes in v2:
time: 107 us
  Pallas kernels  53.9 us (50%)
  waiting for transfers between devices  26.9 us (25%)
  between operations  13.4 us (13%)
  local copies, waits for them, and re-layouts  12.9 us (12%)
    pallas_call x1, Pallas kernels, reduce_update(): pl.pallas_call(reduce_kernel, out_shape=jax.ShapeDtypeStruct(references.s...  29.1 us
    all_gather x1, waiting for transfers between devices, local(): refs = lax.all_gather(references, ('cls', 'rep'), axis=0, tiled=False)  26.2 us
    pallas_call x1, Pallas kernels, filter_tiles(): pl.pallas_call(filter_kernel, grid_spec=grid_spec, out_shape=jax.ShapeDty...  16.3 us
    unnamed x23, local copies, waits for them, and re-layouts  12.9 us
    pallas_call x1, Pallas kernels, weigh(): pl.pallas_call(weigh_kernel, grid_spec=grid_spec, out_shape=[jax.ShapeDty...  8.48 us
  transfers between devices with their start and end apart: 1, of which 1 were waited for; matrix products, arithmetic and copies ran while one was open for 0% of the time, Pallas kernels for 15%

profile of v2, /device:TPU:0, one launch (start us, length us, event | category | flops | bytes accessed | tf_op | source)
XLA Modules:
  0.0 107.2 jit_solution(16167321160241324806)
XLA Ops:
  6.5 0.0 all-gather.3.cloned.1.call-start
  6.5 0.7 all-gather.3.cloned.1.call-update
  7.3 0.0 copy-start.5
  7.3 2.2 %copy-done.5 = bf16[32,256,256]{2,1,0:T(8,128)(2,1)S(1)} copy-done((bf16[32,256,256]{2,1,0:T(8,128)(2,1)S(1)}, bf16[32,256,256]{2,1,0:T(8,128)(2,1)}, u32[]{:S(2)}) %copy-start.5) | copy-done | bytes 4194328
  9.4 0.0 copy-start.6
  9.4 1.0 copy-done.6
  10.5 0.0 copy-start.7
  10.5 0.7 copy-done.7
  11.1 0.0 copy-start.8
  11.1 0.7 copy-done.8
  11.8 0.0 copy-start.9
  11.8 0.7 copy-done.9
  12.5 0.0 copy-start.10
  12.5 0.9 copy-done.10
  13.4 0.0 copy-start.4
  13.4 0.0 copy-start.3
  13.4 16.3 %filter_tiles.1.tile_ref = bf16[32,256,256]{2,1,0:T(8,128)(2,1)S(1)} custom-call(s32[32]{0:T(128)S(1)} %copy-done.7, s32[32]{0:T(128)S(1)} %copy-done.8, f32[31]{0:T(128)S(1)} %copy-done.9, f32[256,256]{1,0:T(8,128)S(1)} %copy-done.10, bf16[4,256,256]{2,1,0:T(8,128)(2,1)S(1)} %copy-done.6, bf16[32,256,256]{2,1,0:T(8,128)(2,1)S(1)} %copy-done.5), custom_call_target="tpu_custom_call" | custom-call | flops 4294967296 | bytes 8388608 | tf_op jit(solution)/shard_map/filter_tiles/pallas_call | solution.py:87
  29.7 0.0 copy-start
  29.7 1.9 %copy-done = bf16[32,256,256]{2,1,0:T(8,128)(2,1)} copy-done((bf16[32,256,256]{2,1,0:T(8,128)(2,1)}, bf16[32,256,256]{2,1,0:T(8,128)(2,1)S(1)}, u32[]{:S(2)}) %copy-start) | copy-done | bytes 4194328
  31.7 26.2 %all-gather.3.cloned.1.call-done = bf16[96,64,256]{2,1,0:T(8,128)(2,1)} async-done(((bf16[6,64,256]{2,1,0:T(8,128)(2,1)}), bf16[96,64,256]{2,1,0:T(8,128)(2,1)}) %all-gather.3.cloned.1.call-update) | async-done | bytes 3145744 | tf_op jit(solution)/shard_map/all_gather | solution.py:337
  57.8 0.0 copy-done.4
  57.8 0.0 copy-start.1
  57.8 2.2 %copy-done.1 = bf16[32,256,256]{2,1,0:T(8,128)(2,1)S(1)} copy-done((bf16[32,256,256]{2,1,0:T(8,128)(2,1)S(1)}, bf16[32,256,256]{2,1,0:T(8,128)(2,1)}, u32[]{:S(2)}) %copy-start.1) | copy-done | bytes 4194328
  60.0 0.0 copy-start.2
  60.0 1.9 %copy-done.2 = bf16[96,64,256]{2,1,0:T(8,128)(2,1)S(1)} copy-done((bf16[96,64,256]{2,1,0:T(8,128)(2,1)S(1)}, bf16[96,64,256]{2,1,0:T(8,128)(2,1)}, u32[]{:S(2)}) %copy-start.2) | copy-done | bytes 3145752
  61.9 8.5 %weigh_tiles.1 = (bf16[4,2,2,6,64,256]{5,4,3,2,1,0:T(8,128)(2,1)S(1)}, f32[4,8,128]{2,1,0:T(8,128)S(1)}) custom-call(s32[32]{0:T(128)S(1)} %copy-done.4, bf16[32,256,256]{2,1,0:T(8,128)(2,1)S(1)} %copy-done.1, bf16[4,4,6,64,256]{4,3,2,1,0:T(8,128)(2,1)S(1)} %bitcast.1), custom_call_target="tpu_custom_call" | custom-call | tf_op jit(solution)/shard_map/weigh_tiles/pallas_call | solution.py:194
  70.4 0.0 copy-done.3
  70.4 29.1 %reduce_update.1 = f32[6,64,256]{2,1,0:T(8,128)S(1)} custom-call(bf16[4,2,2,6,64,256]{5,4,3,2,1,0:T(8,128)(2,1)S(1)} %get-tuple-element.7.sum_ref, f32[4,8,128]{2,1,0:T(8,128)S(1)} %get-tuple-element.8.weight_ref, bf16[6,64,256]{2,1,0:T(8,128)(2,1)S(1)} %copy-done.3), custom_call_target="tpu_custom_call" | custom-call | tf_op jit(solution)/shard_map/reduce_update/pallas_call | solution.py:301
  99.6 0.7 copy.10
Async XLA Ops:
  6.5 51.3 %all-gather.3.cloned.1.call-start = ((), (), s32[]{:S(2)}) async-start(), calls=%async_computation | async-start | bytes 3342336 | tf_op jit(solution)/shard_map/all_gather | solution.py:337
  7.3 2.2 %copy-start.5 = (bf16[32,256,256]{2,1,0:T(8,128)(2,1)S(1)}, bf16[32,256,256]{2,1,0:T(8,128)(2,1)}, u32[]{:S(2)}) copy-start(bf16[32,256,256]{2,1,0:T(8,128)(2,1)} %tile_ref.1) | copy-start | bytes 12582916
  9.4 1.0 copy-start.6
  10.5 0.7 copy-start.7
  11.1 0.7 copy-start.8
  11.8 0.7 copy-start.9
  12.5 0.9 copy-start.10
  13.4 44.4 %copy-start.4 = (s32[32]{0:T(128)S(1)}, s32[32]{0:T(128)}, u32[]{:S(2)}) copy-start(s32[32]{0:T(128)} %class_ref.1) | copy-start | bytes 388
  13.4 57.0 %copy-start.3 = (bf16[6,64,256]{2,1,0:T(8,128)(2,1)S(1)}, bf16[6,64,256]{2,1,0:T(8,128)(2,1)}, u32[]{:S(2)}) copy-start(bf16[6,64,256]{2,1,0:T(8,128)(2,1)} %own_ref.1) | copy-start | bytes 589828
  29.7 1.9 %copy-start = (bf16[32,256,256]{2,1,0:T(8,128)(2,1)}, bf16[32,256,256]{2,1,0:T(8,128)(2,1)S(1)}, u32[]{:S(2)}) copy-start(bf16[32,256,256]{2,1,0:T(8,128)(2,1)S(1)} %filter_tiles.1.tile_ref) | copy-start | bytes 12582916
  57.8 2.2 %copy-start.1 = (bf16[32,256,256]{2,1,0:T(8,128)(2,1)S(1)}, bf16[32,256,256]{2,1,0:T(8,128)(2,1)}, u32[]{:S(2)}) copy-start(bf16[32,256,256]{2,1,0:T(8,128)(2,1)} %copy-done) | copy-start | bytes 12582916
  60.0 1.9 %copy-start.2 = (bf16[96,64,256]{2,1,0:T(8,128)(2,1)S(1)}, bf16[96,64,256]{2,1,0:T(8,128)(2,1)}, u32[]{:S(2)}) copy-start(bf16[96,64,256]{2,1,0:T(8,128)(2,1)} %all-gather.3.cloned.1.call-done) | copy-start | bytes 9437188
Sparse Core Ops, SparseCore 0:
  9.6 48.1 all-gather.2

commit v3 on v2

--- a/solution.py
+++ b/solution.py
@@ -23,16 +23,111 @@
     return (np.cos(phases) + np.sin(phases)).astype(np.float32)
 
 
+def remote(src, dst, send, recv, device):
+    return pltpu.make_async_remote_copy(
+        src_ref=src,
+        dst_ref=dst,
+        send_sem=send,
+        recv_sem=recv,
+        device_id=device,
+        device_id_type=pl.DeviceIdType.MESH,
+    )
+
+
+def enter(devices):
+    barrier = pltpu.get_barrier_semaphore()
+    for device in devices:
+        pl.semaphore_signal(
+            barrier, inc=1, device_id=device, device_id_type=pl.DeviceIdType.MESH
+        )
+    pl.semaphore_wait(barrier, len(devices))
+
+
+def gather_steps(own_ref, all_ref, sems):
+    keep, z_send, z_recv, x_send, x_recv, t_send, t_recv = sems
+    owners, lanes, chips = all_ref.shape[:3]
+    me_z = lax.axis_index("cls")
+    rep = lax.axis_index("rep")
+    me_x, lane = rep // lanes, rep % lanes
+    twin = {"rep": me_x * lanes + (1 - lane)}
+    next_x = [(me_x + d) % chips for d in range(1, chips)]
+    from_z = [(me_z + owners - d) % owners for d in range(1, owners)]
+    to_z = [(me_z + d) % owners for d in range(1, owners)]
+    held = all_ref.at[me_z, lane, me_x]
+
+    def to_x(x):
+        return {"rep": x * lanes + lane}
+
+    def across_z(z, slot):
+        return remote(own_ref, all_ref.at[slot, lane, me_x], z_send.at[z], z_recv.at[slot], {"cls": z})
+
+    def across_x(src, x, z, slot):
+        return remote(src, all_ref.at[z, lane, slot], x_send.at[x, z], x_recv.at[slot, z], to_x(x))
+
+    def across_twin(src, z, x):
+        return remote(src, all_ref.at[z, lane, x], t_send.at[x, z], t_recv.at[x, z], twin)
+
+    def begin():
+        enter([twin] + [to_x(x) for x in next_x] + [{"cls": z} for z in to_z])
+        pltpu.make_async_copy(own_ref, held, keep).start()
+        for z in to_z:
+            across_z(z, me_z).start()
+        for x in next_x:
+            across_x(own_ref, x, me_z, me_x).start()
+        across_twin(own_ref, me_z, me_x).start()
+
+    def pass_z(z):
+        across_z(z, z).wait_recv()
+        src = all_ref.at[z, lane, me_x]
+        for x in next_x:
+            across_x(src, x, z, me_x).start()
+        across_twin(src, z, me_x).start()
+
+    def pass_x(z):
+        for x in next_x:
+            across_x(own_ref, x, z, x).wait_recv()
+            across_twin(all_ref.at[z, lane, x], z, x).start()
+
+    def finish():
+        pltpu.make_async_copy(own_ref, held, keep).wait()
+        for z in [me_z] + from_z:
+            for x in [me_x] + next_x:
+                remote(
+                    own_ref, all_ref.at[z, 1 - lane, x], t_send.at[x, z], t_recv.at[x, z], twin
+                ).wait()
+            for x in next_x:
+                across_x(own_ref, x, z, me_x).wait_send()
+        for z in to_z:
+            across_z(z, me_z).wait_send()
+
+    stages = [begin]
+    for d, z in enumerate(from_z):
+        stages.append(functools.partial(pass_z, z))
+        stages.append(functools.partial(pass_x, me_z if d == 0 else from_z[d - 1]))
+    stages.append(functools.partial(pass_x, from_z[-1]))
+    stages.append(finish)
+    return stages
+
+
 def filter_kernel(
-    turn_ref, bin_ref, taps_ref, hartley_ref, ctf_ref, tile_ref, out_ref, fwd, fwd_t, syn
+    turn_ref, bin_ref, taps_ref, hartley_ref, ctf_ref, tile_ref, *rest
 ):
+    if len(rest) > 4:
+        own_ref, out_ref, all_ref, fwd, fwd_t, syn = rest[:6]
+        stages = gather_steps(own_ref, all_ref, rest[6:])
+    else:
+        out_ref, fwd, fwd_t, syn = rest
+        stages = []
     batch, tile_len, _ = tile_ref.shape
     taps = taps_ref.shape[0]
     half = (taps - 1) // 2
     step = pl.program_id(0)
+    steps = pl.num_programs(0)
 
     @pl.when(step == 0)
     def _():
+        if stages:
+            stages[0]()
         row = lax.broadcasted_iota(jnp.int32, (tile_len, tile_len), 0)
         col = lax.broadcasted_iota(jnp.int32, (tile_len, tile_len), 1)
         gap = col - row
@@ -63,45 +158,70 @@
         result = jnp.dot(syn[...], second, preferred_element_type=F32)
         out_ref[i] = (result * (1.0 / (tile_len * tile_len))).astype(BF16)
 
-
-def filter_tiles(particles, rotation, defocus, filter_taps, ctf_table):
+    for at, stage in enumerate(stages[1:]):
+
+        @pl.when(step == jnp.minimum(at + 1, steps - 1))
+        def _(stage=stage):
+            stage()
+
+
+def filter_tiles(particles, rotation, defocus, filter_taps, ctf_table, references, gather):
     count, tile_len, _ = particles.shape
     batch = math.gcd(count, 4)
     hartley = jnp.asarray(hartley_table(tile_len))
     square = (tile_len, tile_len)
-    grid_spec = pltpu.PrefetchScalarGridSpec(
-        num_scalar_prefetch=3,
-        grid=(count // batch,),
-        in_specs=[
-            pl.BlockSpec(square, lambda i, *_: (0, 0)),
-            pl.BlockSpec(ctf_table.shape, lambda i, *_: (0, 0, 0)),
-            pl.BlockSpec((batch,) + square, lambda i, *_: (i, 0, 0)),
-        ],
-        out_specs=pl.BlockSpec((batch,) + square, lambda i, *_: (i, 0, 0)),
-        scratch_shapes=[
-            pltpu.VMEM((2,) + square, BF16),
-            pltpu.VMEM((2,) + square, BF16),
-            pltpu.VMEM(square, BF16),
-        ],
-    )
+    in_specs = [pl.BlockSpec(memory_space=pltpu.SMEM)] * 3 + [
+        pl.BlockSpec(square, lambda i: (0, 0)),
+        pl.BlockSpec(ctf_table.shape, lambda i: (0, 0, 0)),
+        pl.BlockSpec((batch,) + square, lambda i: (i, 0, 0)),
+    ]
+    out_specs = [pl.BlockSpec((batch,) + square, lambda i: (i, 0, 0))]
+    out_shape = [jax.ShapeDtypeStruct(particles.shape, BF16)]
+    scratch = [
+        pltpu.VMEM((2,) + square, BF16),
+        pltpu.VMEM((2,) + square, BF16),
+        pltpu.VMEM(square, BF16),
+    ]
+    operands = [rotation, defocus, filter_taps, hartley, ctf_table, particles]
+    params = dict(vmem_limit_bytes=56 * MIB)
+    if gather:
+        owners, lanes, chips = gather
+        dma = pltpu.SemaphoreType.DMA
+        in_specs.append(pl.BlockSpec(memory_space=pl.ANY))
+        out_specs.append(pl.BlockSpec(memory_space=pl.ANY))
+        out_shape.append(jax.ShapeDtypeStruct(gather + references.shape, BF16))
+        scratch += [
+            dma,
+            dma((owners,)),
+            dma((owners,)),
+            dma((chips, owners)),
+            dma((chips, owners)),
+            dma((chips, owners)),
+            dma((chips, owners)),
+        ]
+        operands.append(references)
+        params.update(collective_id=2, has_side_effects=True)
     return pl.pallas_call(
         filter_kernel,
-        grid_spec=grid_spec,
-        out_shape=jax.ShapeDtypeStruct(particles.shape, BF16),
-        compiler_params=pltpu.CompilerParams(vmem_limit_bytes=24 * MIB),
+        grid=(count // batch,),
+        in_specs=in_specs,
+        out_specs=out_specs,
+        scratch_shapes=scratch,
+        out_shape=out_shape,
+        compiler_params=pltpu.CompilerParams(**params),
         cost_estimate=pl.CostEstimate(
             flops=8 * count * tile_len**3,
             bytes_accessed=4 * count * tile_len**2,
             transcendentals=0,
         ),
         name="filter_tiles",
-    )(rotation, defocus, filter_taps, hartley, ctf_table, particles)
+    )(*operands)
 
 
 def weigh_kernel(class_ref, tile_ref, refs_ref, sum_ref, weight_ref, acc, start, order):
     count, tile_len, _ = tile_ref.shape
-    _, reps, own, rows, _ = refs_ref.shape
-    lanes = sum_ref.shape[1]
+    _, lanes, chips, own, rows, _ = refs_ref.shape
+    reps = lanes * chips
     owners = pl.num_programs(0)
     owner = pl.program_id(0)
     scale = 1.0 / (tile_len * tile_len)
@@ -150,7 +270,9 @@
         p = order[i]
         k = class_ref[p] - owner * own
         tile = tile_ref[p].astype(F32)
-        image = refs_ref[0, :, k].reshape(tile_len, tile_len).astype(F32)
+        image = jnp.concatenate(
+            [refs_ref[0, rep % lanes, rep // lanes, k] for rep in range(reps)], axis=0
+        ).astype(F32)
         power = total(tile * tile) * scale
         ref_power = total(image * image) * scale
         meet = total(tile * image) * scale
@@ -168,21 +290,20 @@
             sum_ref[0, rep % lanes, rep // lanes, k] = whole[rep]
 
 
-def weigh(filtered, classes, refs, lanes):
+def weigh(filtered, classes, refs):
     count, tile_len, _ = filtered.shape
-    owners, reps, own, rows, _ = refs.shape
+    owners, lanes, chips, own, rows, _ = refs.shape
     slots = -(-own // 8) * 8
-    block = (1, reps, own, rows, tile_len)
-    parted = (owners, lanes, reps // lanes, own, rows, tile_len)
+    block = (1,) + refs.shape[1:]
     grid_spec = pltpu.PrefetchScalarGridSpec(
         num_scalar_prefetch=1,
         grid=(owners,),
         in_specs=[
             pl.BlockSpec(filtered.shape, lambda o, *_: (0, 0, 0)),
-            pl.BlockSpec(block, lambda o, *_: (o, 0, 0, 0, 0)),
+            pl.BlockSpec(block, lambda o, *_: (o, 0, 0, 0, 0, 0)),
         ],
         out_specs=[
-            pl.BlockSpec((1,) + parted[1:], lambda o, *_: (o, 0, 0, 0, 0, 0)),
+            pl.BlockSpec(block, lambda o, *_: (o, 0, 0, 0, 0, 0)),
             pl.BlockSpec((1, slots, 128), lambda o, *_: (o, 0, 0)),
         ],
         scratch_shapes=[
@@ -195,10 +316,10 @@
         weigh_kernel,
         grid_spec=grid_spec,
         out_shape=[
-            jax.ShapeDtypeStruct(parted, BF16),
+            jax.ShapeDtypeStruct(refs.shape, BF16),
             jax.ShapeDtypeStruct((owners, slots, 128), F32),
         ],
-        compiler_params=pltpu.CompilerParams(vmem_limit_bytes=32 * MIB),
+        compiler_params=pltpu.CompilerParams(vmem_limit_bytes=56 * MIB),
         name="weigh_tiles",
     )(classes, filtered, refs)
 
@@ -334,14 +455,18 @@
     owners = lax.axis_size("cls")
     reps = lax.axis_size("rep")
     own, rows, tile_len = references.shape
+    stack = (owners, 2, reps // 2)
+    small = reps % 2 == 0 and owners * reps * references.size <= 4 * MIB
+    tiles = (particles, rotation, defocus, filter_taps, ctf_table, references)
+    if small:
+        filtered, refs = filter_tiles(*tiles, stack)
+        sums, weights = weigh(filtered, classes, refs)
+        return reduce_update(sums, weights, references)
     refs = lax.all_gather(references, ("cls", "rep"), axis=0, tiled=False)
-    refs = refs.reshape(owners, reps, own, rows, tile_len)
-    filtered = filter_tiles(particles, rotation, defocus, filter_taps, ctf_table)
-    small = reps % 2 == 0 and refs.size <= 4 * MIB
-    sums, weights = weigh(filtered, classes, refs, 2 if small else 1)
-    if small:
-        return reduce_update(sums, weights, references)
-    sums = sums.reshape(refs.shape)
+    [filtered] = filter_tiles(*tiles, None)
+    refs = refs.reshape(owners, 1, reps, own, rows, tile_len)
+    sums, weights = weigh(filtered, classes, refs)
+    sums = sums[:, 0]
     sums = lax.psum_scatter(sums, "rep", scatter_dimension=1, tiled=False)
     sums = lax.psum_scatter(sums, "cls", scatter_dimension=0, tiled=False)
     weights = lax.psum(weights[:, :own, 0], ("cls", "rep"))

time: 107 us -> 82.8 us (0.77)
  waiting for transfers between devices: 26.9 us -> 0 us
  Pallas kernels: 53.9 us -> 79.1 us
  between operations: 13.4 us -> 0.03 us
  local copies, waits for them, and re-layouts: 12.9 us -> 3.36 us
    all_gather x1 -> x0, waiting for transfers between devices: 26.2 us -> none  [local(): refs = lax.all_gather(references, ('cls', 'rep'), axis=0, tiled=False)]
    pallas_call x1, Pallas kernels: 16.3 us -> 33.7 us  [filter_tiles(): pl.pallas_call(filter_kernel, grid=(count // batch,), in_specs=in_specs,...]
    unnamed x23 -> x7, local copies, waits for them, and re-layouts: 12.9 us -> 3.36 us
    pallas_call x1, Pallas kernels: 8.48 us -> 13.4 us  [weigh(): pl.pallas_call(weigh_kernel, grid_spec=grid_spec, out_shape=[jax.ShapeDty...]
    pallas_call x1, Pallas kernels: 29.1 us -> 31.9 us  [reduce_update(): pl.pallas_call(reduce_kernel, out_shape=jax.ShapeDtypeStruct(references.s...]
  transfers between devices with their start and end apart: 1 -> 0, of which waited for: 1 -> 0; matrix products, arithmetic and copies ran while one was open for 0% -> 0% of each run, Pallas kernels for 15% -> 0%
where the time goes in v3:
time: 82.8 us; the launch traced here: 82.4 us
  Pallas kernels  79.1 us (96%)
  local copies, waits for them, and re-layouts  3.36 us (4%)
    pallas_call x1, Pallas kernels, filter_tiles(): pl.pallas_call(filter_kernel, grid=(count // batch,), in_specs=in_specs,...  33.7 us
    pallas_call x1, Pallas kernels, reduce_update(): pl.pallas_call(reduce_kernel, out_shape=jax.ShapeDtypeStruct(references.s...  31.9 us
    pallas_call x1, Pallas kernels, weigh(): pl.pallas_call(weigh_kernel, grid_spec=grid_spec, out_shape=[jax.ShapeDty...  13.4 us
    unnamed x7, local copies, waits for them, and re-layouts  3.36 us

profile of v3, /device:TPU:0, one launch (start us, length us, event | category | flops | bytes accessed | tf_op | source)
XLA Modules:
  0.0 82.4 jit_solution(8190353745907460886)
XLA Ops:
  0.0 33.7 %filter_tiles.1 = (bf16[32,256,256]{2,1,0:T(8,128)(2,1)}, bf16[4,2,2,6,64,256]{5,4,3,2,1,0:T(8,128)(2,1)}) custom-call(s32[32]{0:T(128)} %turn_ref.1, s32[32]{0:T(128)} %bin_ref.1, f32[31]{0:T(128)} %taps_ref.1, f32[256,256]{1,0:T(8,128)} %constant.2.clone.hartley_ref, bf16[4,256,256]{2,1,0:T(8,128)(2,1)} %ctf_ref.1, bf16[32,256,256]{2,1,0:T(8,128)(2,1)} %tile_ref.1, ...), custom_call_target="tpu_custom_call" | custom-call | flops 4294967296 | bytes 8388608 | tf_op jit(solution)/shard_map/filter_tiles/pallas_call | solution.py:204
  33.8 0.0 copy-start.1
  33.8 13.4 %weigh_tiles.1 = (bf16[4,2,2,6,64,256]{5,4,3,2,1,0:T(8,128)(2,1)}, f32[4,8,128]{2,1,0:T(8,128)}) custom-call(s32[32]{0:T(128)} %class_ref.1, bf16[32,256,256]{2,1,0:T(8,128)(2,1)} %get-tuple-element.9.tile_ref, bf16[4,2,2,6,64,256]{5,4,3,2,1,0:T(8,128)(2,1)} %get-tuple-element.10.refs_ref), custom_call_target="tpu_custom_call" | custom-call | tf_op jit(solution)/shard_map/weigh_tiles/pallas_call | solution.py:315
  47.1 0.0 copy-done.1
  47.1 0.0 copy-start
  47.1 1.9 %copy-done = bf16[4,2,2,6,64,256]{5,4,3,2,1,0:T(8,128)(2,1)S(1)} copy-done((bf16[4,2,2,6,64,256]{5,4,3,2,1,0:T(8,128)(2,1)S(1)}, bf16[4,2,2,6,64,256]{5,4,3,2,1,0:T(8,128)(2,1)}, u32[]{:S(2)}) %copy-start) | copy-done | bytes 3145752
  49.0 0.0 copy-start.2
  49.0 0.7 copy-done.2
  49.7 31.9 %reduce_update.1 = f32[6,64,256]{2,1,0:T(8,128)S(1)} custom-call(bf16[4,2,2,6,64,256]{5,4,3,2,1,0:T(8,128)(2,1)S(1)} %copy-done, f32[4,8,128]{2,1,0:T(8,128)S(1)} %copy-done.2, bf16[6,64,256]{2,1,0:T(8,128)(2,1)S(1)} %copy-done.1), custom_call_target="tpu_custom_call" | custom-call | tf_op jit(solution)/shard_map/reduce_update/pallas_call | solution.py:422
  81.7 0.7 copy.10
Async XLA Ops:
  33.8 13.4 %copy-start.1 = (bf16[6,64,256]{2,1,0:T(8,128)(2,1)S(1)}, bf16[6,64,256]{2,1,0:T(8,128)(2,1)}, u32[]{:S(2)}) copy-start(bf16[6,64,256]{2,1,0:T(8,128)(2,1)} %own_ref.1) | copy-start | bytes 589828
  47.1 1.9 %copy-start = (bf16[4,2,2,6,64,256]{5,4,3,2,1,0:T(8,128)(2,1)S(1)}, bf16[4,2,2,6,64,256]{5,4,3,2,1,0:T(8,128)(2,1)}, u32[]{:S(2)}) copy-start(bf16[4,2,2,6,64,256]{5,4,3,2,1,0:T(8,128)(2,1)} %get-tuple-element.11.sum_ref) | copy-start | bytes 9437188
  49.0 0.7 copy-start.2

commit v4 on v3

--- a/solution.py
+++ b/solution.py
@@ -51,15 +51,20 @@
     me_x, lane = rep // lanes, rep % lanes
     twin = {"rep": me_x * lanes + (1 - lane)}
     next_x = [(me_x + d) % chips for d in range(1, chips)]
-    from_z = [(me_z + owners - d) % owners for d in range(1, owners)]
-    to_z = [(me_z + d) % owners for d in range(1, owners)]
     held = all_ref.at[me_z, lane, me_x]
+    has_left, has_right = me_z > 0, me_z < owners - 1
 
     def to_x(x):
         return {"rep": x * lanes + lane}
 
-    def across_z(z, slot):
-        return remote(own_ref, all_ref.at[slot, lane, me_x], z_send.at[z], z_recv.at[slot], {"cls": z})
+    def along_z(src, z, way):
+        return remote(
+            src,
+            all_ref.at[z, lane, me_x],
+            z_send.at[way, z],
+            z_recv.at[z],
+            {"cls": me_z + 1 if way else me_z - 1},
+        )
 
     def across_x(src, x, z, slot):
         return remote(src, all_ref.at[z, lane, slot], x_send.at[x, z], x_recv.at[slot, z], to_x(x))
@@ -68,45 +73,64 @@
         return remote(src, all_ref.at[z, lane, x], t_send.at[x, z], t_recv.at[x, z], twin)
 
     def begin():
-        enter([twin] + [to_x(x) for x in next_x] + [{"cls": z} for z in to_z])
-        pltpu.make_async_copy(own_ref, held, keep).start()
-        for z in to_z:
-            across_z(z, me_z).start()
+        others = [{"cls": (me_z + d) % owners} for d in range(1, owners)]
+        enter([twin] + [to_x(x) for x in next_x] + others)
+        pl.when(has_right)(lambda: along_z(own_ref, me_z, 1).start())
+        pl.when(has_left)(lambda: along_z(own_ref, me_z, 0).start())
         for x in next_x:
             across_x(own_ref, x, me_z, me_x).start()
         across_twin(own_ref, me_z, me_x).start()
-
-    def pass_z(z):
-        across_z(z, z).wait_recv()
-        src = all_ref.at[z, lane, me_x]
-        for x in next_x:
-            across_x(src, x, z, me_x).start()
-        across_twin(src, z, me_x).start()
+        pltpu.make_async_copy(own_ref, held, keep).start()
+
+    def sides(distance):
+        low, high = me_z - distance, me_z + distance
+        return [(low >= 0, low, has_right, 1), (high < owners, high, has_left, 0)]
+
+    def pass_z(distance):
+        for there, z, onward, way in sides(distance):
+
+            @pl.when(there)
+            def _(z=z, onward=onward, way=way):
+                src = all_ref.at[z, lane, me_x]
+                along_z(own_ref, z, way).wait_recv()
+                pl.when(onward)(lambda: along_z(src, z, way).start())
+                for x in next_x:
+                    across_x(src, x, z, me_x).start()
+                across_twin(src, z, me_x).start()
 
     def pass_x(z):
         for x in next_x:
             across_x(own_ref, x, z, x).wait_recv()
             across_twin(all_ref.at[z, lane, x], z, x).start()
 
+    def pass_x_side(distance, side):
+        there, z, _, _ = sides(distance)[side]
+        pl.when(there)(lambda: pass_x(z))
+
     def finish():
         pltpu.make_async_copy(own_ref, held, keep).wait()
-        for z in [me_z] + from_z:
+        for z in range(owners):
             for x in [me_x] + next_x:
                 remote(
                     own_ref, all_ref.at[z, 1 - lane, x], t_send.at[x, z], t_recv.at[x, z], twin
                 ).wait()
             for x in next_x:
                 across_x(own_ref, x, z, me_x).wait_send()
-        for z in to_z:
-            across_z(z, me_z).wait_send()
-
-    stages = [begin]
-    for d, z in enumerate(from_z):
-        stages.append(functools.partial(pass_z, z))
-        stages.append(functools.partial(pass_x, me_z if d == 0 else from_z[d - 1]))
-    stages.append(functools.partial(pass_x, from_z[-1]))
-    stages.append(finish)
-    return stages
+        pl.when(has_right)(lambda: along_z(own_ref, me_z, 1).wait_send())
+        pl.when(has_left)(lambda: along_z(own_ref, me_z, 0).wait_send())
+        for distance in range(1, owners):
+            for there, z, onward, way in sides(distance):
+                pl.when(there & onward)(
+                    functools.partial(lambda z, way: along_z(own_ref, z, way).wait_send(), z, way)
+                )
+
+    stages = [(0, begin), (5, functools.partial(pass_x, me_z))]
+    for d in range(1, owners):
+        stages.append((4 * d, functools.partial(pass_z, d)))
+        stages.append((4 * d + 5, functools.partial(pass_x_side, d, 0)))
+        stages.append((4 * d + 7, functools.partial(pass_x_side, d, 1)))
+    stages.sort(key=lambda entry: entry[0])
+    return stages + [(1 << 20, finish)]
 
 
 def filter_kernel(
@@ -127,7 +151,7 @@
     @pl.when(step == 0)
     def _():
         if stages:
-            stages[0]()
+            stages[0][1]()
         row = lax.broadcasted_iota(jnp.int32, (tile_len, tile_len), 0)
         col = lax.broadcasted_iota(jnp.int32, (tile_len, tile_len), 1)
         gap = col - row
@@ -158,16 +182,16 @@
         result = jnp.dot(syn[...], second, preferred_element_type=F32)
         out_ref[i] = (result * (1.0 / (tile_len * tile_len))).astype(BF16)
 
-    for at, stage in enumerate(stages[1:]):
-
-        @pl.when(step == jnp.minimum(at + 1, steps - 1))
+    for at, stage in stages[1:]:
+
+        @pl.when(step == jnp.minimum(at, steps - 1))
         def _(stage=stage):
             stage()
 
 
 def filter_tiles(particles, rotation, defocus, filter_taps, ctf_table, references, gather):
     count, tile_len, _ = particles.shape
-    batch = math.gcd(count, 4)
+    batch = math.gcd(count, 2)
     hartley = jnp.asarray(hartley_table(tile_len))
     square = (tile_len, tile_len)
     in_specs = [pl.BlockSpec(memory_space=pltpu.SMEM)] * 3 + [
@@ -192,7 +216,7 @@
         out_shape.append(jax.ShapeDtypeStruct(gather + references.shape, BF16))
         scratch += [
             dma,
-            dma((owners,)),
+            dma((2, owners)),
             dma((owners,)),
             dma((chips, owners)),
             dma((chips, owners)),
@@ -326,7 +350,7 @@
 
 def reduce_kernel(
     sum_ref, weight_ref, own_ref, out_ref, near, far, share, deep, w_near, w_far, w_share, w_deep,
-    near_sem, far_send, far_recv, deep_send, deep_recv, wn_sem, wf_send, wf_recv, wd_send, wd_recv
+    kept, keep, near_sem, far_send, far_recv, deep_send, deep_recv, wn_sem, wf_send, wf_recv, wd_send, wd_recv
 ):
     owners, lanes, chips, own, rows, _ = sum_ref.shape
     me_z = lax.axis_index("cls")
@@ -367,6 +391,8 @@
     for o in order:
         launch(copy(sum_ref.at[o, 1 - lane], near.at[o], near_sem.at[0, o], near_sem.at[1, o], twin))
 
+    for o in order:
+        pltpu.make_async_copy(sum_ref.at[o, lane], kept.at[o], keep.at[o]).start()
     copy(weight_ref, w_near, wn_sem.at[0], wn_sem.at[1], twin).wait_recv()
     w_share[...] = weight_ref[...] + w_near[...]
     for x in peers_x:
@@ -375,7 +401,8 @@
         copy(
             sum_ref.at[o, lane], near.at[o], near_sem.at[0, o], near_sem.at[1, o], twin
         ).wait_recv()
-        near[o] = (near[o].astype(F32) + sum_ref[o, lane].astype(F32)).astype(BF16)
+        pltpu.make_async_copy(sum_ref.at[o, lane], kept.at[o], keep.at[o]).wait()
+        near[o] = (near[o].astype(F32) + kept[o].astype(F32)).astype(BF16)
         for x in peers_x:
             launch(
                 copy(near.at[o, x], far.at[me_x, o], far_send.at[x, o], far_recv.at[me_x, o], to_x(x))
@@ -422,7 +449,7 @@
     return pl.pallas_call(
         reduce_kernel,
         out_shape=jax.ShapeDtypeStruct(references.shape, F32),
-        in_specs=[pl.BlockSpec(memory_space=pltpu.VMEM)] * 3,
+        in_specs=[pl.BlockSpec(memory_space=pl.ANY)] + [pl.BlockSpec(memory_space=pltpu.VMEM)] * 2,
         out_specs=pl.BlockSpec(memory_space=pltpu.VMEM),
         scratch_shapes=[
             pltpu.VMEM((owners, chips) + piece, BF16),
@@ -433,6 +460,8 @@
             pltpu.VMEM((chips, owners) + slots, F32),
             pltpu.VMEM((owners,) + slots, F32),
             pltpu.VMEM((owners,) + slots, F32),
+            pltpu.VMEM((owners, chips) + piece, BF16),
+            dma((owners,)),
             dma((2, owners)),
             dma((chips, owners)),
             dma((chips, owners)),
@@ -445,7 +474,7 @@
             dma((owners,)),
         ],
         compiler_params=pltpu.CompilerParams(
-            collective_id=1, has_side_effects=True, vmem_limit_bytes=32 * MIB
+            collective_id=1, has_side_effects=True, vmem_limit_bytes=56 * MIB
         ),
         name="reduce_update",
     )(sums, weights, references)

time: 82.8 us -> 77.5 us (0.936)
  Pallas kernels: 79.1 us -> 75.9 us
  local copies, waits for them, and re-layouts: 3.36 us -> 1.78 us
    unnamed x7 -> x1, local copies, waits for them, and re-layouts: 3.36 us -> 1.78 us
    pallas_call x1, Pallas kernels: 13.4 us -> 11.9 us  [weigh(): pl.pallas_call(weigh_kernel, grid_spec=grid_spec, out_shape=[jax.ShapeDty...]
    pallas_call x1, Pallas kernels: 33.7 us -> 32.6 us  [filter_tiles(): pl.pallas_call(filter_kernel, grid=(count // batch,), in_specs=in_specs,...]
where the time goes in v4:
time: 77.5 us; the launch traced here: 77.7 us
  Pallas kernels  75.9 us (98%)
  local copies, waits for them, and re-layouts  1.78 us (2%)
    pallas_call x1, Pallas kernels, filter_tiles(): pl.pallas_call(filter_kernel, grid=(count // batch,), in_specs=in_specs,...  32.6 us
    pallas_call x1, Pallas kernels, reduce_update(): pl.pallas_call(reduce_kernel, out_shape=jax.ShapeDtypeStruct(references.s...  31.4 us
    pallas_call x1, Pallas kernels, weigh(): pl.pallas_call(weigh_kernel, grid_spec=grid_spec, out_shape=[jax.ShapeDty...  11.9 us
    unnamed x1, local copies, waits for them, and re-layouts  1.78 us

profile of v4, /device:TPU:0, one launch (start us, length us, event | category | flops | bytes accessed | tf_op | source)
XLA Modules:
  0.0 77.7 jit_solution(15150939938733142040)
XLA Ops:
  0.0 32.6 %filter_tiles.1 = (bf16[32,256,256]{2,1,0:T(8,128)(2,1)}, bf16[4,2,2,6,64,256]{5,4,3,2,1,0:T(8,128)(2,1)}) custom-call(s32[32]{0:T(128)} %turn_ref.1, s32[32]{0:T(128)} %bin_ref.1, f32[31]{0:T(128)} %taps_ref.1, f32[256,256]{1,0:T(8,128)} %constant.2.clone.hartley_ref, bf16[4,256,256]{2,1,0:T(8,128)(2,1)} %ctf_ref.1, bf16[32,256,256]{2,1,0:T(8,128)(2,1)} %tile_ref.1, ...), custom_call_target="tpu_custom_call" | custom-call | flops 4294967296 | bytes 8388608 | tf_op jit(solution)/shard_map/filter_tiles/pallas_call | solution.py:228
  32.6 11.9 %weigh_tiles.1 = (bf16[4,2,2,6,64,256]{5,4,3,2,1,0:T(8,128)(2,1)}, f32[4,8,128]{2,1,0:T(8,128)}) custom-call(s32[32]{0:T(128)} %class_ref.1, bf16[32,256,256]{2,1,0:T(8,128)(2,1)} %get-tuple-element.9.tile_ref, bf16[4,2,2,6,64,256]{5,4,3,2,1,0:T(8,128)(2,1)} %get-tuple-element.10.refs_ref), custom_call_target="tpu_custom_call" | custom-call | tf_op jit(solution)/shard_map/weigh_tiles/pallas_call | solution.py:339
  44.5 31.4 %reduce_update.1 = f32[6,64,256]{2,1,0:T(8,128)} custom-call(bf16[4,2,2,6,64,256]{5,4,3,2,1,0:T(8,128)(2,1)} %get-tuple-element.11.sum_ref, f32[4,8,128]{2,1,0:T(8,128)} %get-tuple-element.12.weight_ref, bf16[6,64,256]{2,1,0:T(8,128)(2,1)} %own_ref.1), custom_call_target="tpu_custom_call" | custom-call | tf_op jit(solution)/shard_map/reduce_update/pallas_call | solution.py:449
  75.9 1.8 %copy.10 = f32[6,64,256]{2,1,0:T(8,128)} copy(f32[6,64,256]{2,1,0:T(8,128)} %reduce_update.1) | data formatting | bytes 786432

commit v5 on v4

--- a/solution.py
+++ b/solution.py
@@ -242,7 +242,10 @@
     )(*operands)
 
 
-def weigh_kernel(class_ref, tile_ref, refs_ref, sum_ref, weight_ref, acc, start, order):
+def weigh_kernel(
+    class_ref, tile_ref, refs_ref, sum_ref, weight_ref, acc, parts, weigh_by, scale_by,
+    start, order
+):
     count, tile_len, _ = tile_ref.shape
     _, lanes, chips, own, rows, _ = refs_ref.shape
     reps = lanes * chips
@@ -287,27 +290,49 @@
     weight_ref[...] = jnp.zeros_like(weight_ref)
     row = lax.broadcasted_iota(jnp.int32, weight_ref.shape[1:], 0)
 
-    def total(values):
-        return jnp.sum(jnp.sum(values, axis=0, keepdims=True), axis=1, keepdims=True)
-
-    def body(i, carry):
+    def fold(values):
+        tall = jnp.sum(values.reshape(rows // 8, 8, tile_len), axis=0)
+        return sum(tall[:, at : at + 128] for at in range(0, tile_len, 128))
+
+    def gather_parts(i, carry):
         p = order[i]
         k = class_ref[p] - owner * own
-        tile = tile_ref[p].astype(F32)
-        image = jnp.concatenate(
-            [refs_ref[0, rep % lanes, rep // lanes, k] for rep in range(reps)], axis=0
-        ).astype(F32)
-        power = total(tile * tile) * scale
-        ref_power = total(image * image) * scale
-        meet = total(tile * image) * scale
-        score = meet / jnp.sqrt((power + EPSILON) * (ref_power + EPSILON))
-        weight = 1.0 / (1.0 + jnp.exp(-tile_len * score))
-        scaling = (weight / jnp.sqrt(power + EPSILON)).astype(BF16).astype(F32)
-        acc[k] += scaling * tile
-        weight_ref[0] += jnp.where(row == k, weight, 0.0)
+        power = ref_power = meet = jnp.zeros((8, 128), F32)
+        for rep in range(reps):
+            tile = tile_ref[p, rep * rows : (rep + 1) * rows].astype(F32)
+            image = refs_ref[0, rep % lanes, rep // lanes, k].astype(F32)
+            power = power + fold(tile * tile)
+            ref_power = ref_power + fold(image * image)
+            meet = meet + fold(tile * image)
+        parts[0, i] = power
+        parts[1, i] = ref_power
+        parts[2, i] = meet
         return carry
 
-    lax.fori_loop(begin, end, body, 0)
+    lax.fori_loop(begin, end, gather_parts, 0)
+
+    def total(which):
+        return jnp.sum(jnp.sum(parts[which], axis=1), axis=1, keepdims=True) * scale
+
+    power, ref_power, meet = total(0), total(1), total(2)
+    score = meet / jnp.sqrt((power + EPSILON) * (ref_power + EPSILON))
+    weight = 1.0 / (1.0 + jnp.exp(-tile_len * score))
+    scaling = (weight / jnp.sqrt(power + EPSILON)).astype(BF16).astype(F32)
+    weigh_by[...] = jnp.broadcast_to(weight, weigh_by.shape)
+    scale_by[...] = jnp.broadcast_to(scaling, scale_by.shape)
+
+    def add_tile(i, carry):
+        p = order[i]
+        k = class_ref[p] - owner * own
+        factor = jnp.broadcast_to(scale_by[pl.ds(i, 1), :], (rows, 128))
+        factor = jnp.concatenate([factor] * (tile_len // 128), axis=1)
+        for rep in range(reps):
+            part = pl.ds(rep * rows, rows)
+            acc[k, part] += factor * tile_ref[p, part].astype(F32)
+        weight_ref[0] += jnp.where(row == k, weigh_by[pl.ds(i, 1), :], 0.0)
+        return carry
+
+    lax.fori_loop(begin, end, add_tile, 0)
     for k in range(own):
         whole = acc[k].astype(BF16).reshape(reps, rows, tile_len)
         for rep in range(reps):
@@ -332,6 +357,9 @@
         ],
         scratch_shapes=[
             pltpu.VMEM((own, tile_len, tile_len), F32),
+            pltpu.VMEM((3, count, 8, 128), F32),
+            pltpu.VMEM((count, 128), F32),
+            pltpu.VMEM((count, 128), F32),
             pltpu.SMEM((owners + 1,), jnp.int32),
             pltpu.SMEM((count,), jnp.int32),
         ],
@@ -474,7 +502,7 @@
             dma((owners,)),
         ],
         compiler_params=pltpu.CompilerParams(
-            collective_id=1, has_side_effects=True, vmem_limit_bytes=56 * MIB
+            collective_id=1, has_side_effects=True, vmem_limit_bytes=32 * MIB
         ),
         name="reduce_update",
     )(sums, weights, references)

time: 77.5 us -> 72.9 us (0.941); the launches traced: 77.7 us -> 71.7 us
  Pallas kernels: 75.9 us -> 68.3 us
  local copies, waits for them, and re-layouts: 1.78 us -> 3.36 us
    pallas_call x1, Pallas kernels: 31.4 us -> 26.6 us  [reduce_update(): pl.pallas_call(reduce_kernel, out_shape=jax.ShapeDtypeStruct(references.s...]
    pallas_call x1, Pallas kernels: 11.9 us -> 9.11 us  [weigh(): pl.pallas_call(weigh_kernel, grid_spec=grid_spec, out_shape=[jax.ShapeDty...]
    unnamed x1 -> x7, local copies, waits for them, and re-layouts: 1.78 us -> 3.36 us
where the time goes in v5:
time: 72.9 us; the launch traced here: 71.7 us
  Pallas kernels  68.3 us (94%)
  local copies, waits for them, and re-layouts  3.36 us (5%)
    pallas_call x1, Pallas kernels, filter_tiles(): pl.pallas_call(filter_kernel, grid=(count // batch,), in_specs=in_specs,...  32.6 us
    pallas_call x1, Pallas kernels, reduce_update(): pl.pallas_call(reduce_kernel, out_shape=jax.ShapeDtypeStruct(references.s...  26.6 us
    pallas_call x1, Pallas kernels, weigh(): pl.pallas_call(weigh_kernel, grid_spec=grid_spec, out_shape=[jax.ShapeDty...  9.11 us
    unnamed x7, local copies, waits for them, and re-layouts  3.36 us

profile of v5, /device:TPU:0, one launch (start us, length us, event | category | flops | bytes accessed | tf_op | source)
XLA Modules:
  0.0 71.7 jit_solution(15212575676007827728)
XLA Ops:
  0.0 32.6 %filter_tiles.1 = (bf16[32,256,256]{2,1,0:T(8,128)(2,1)}, bf16[4,2,2,6,64,256]{5,4,3,2,1,0:T(8,128)(2,1)}) custom-call(s32[32]{0:T(128)} %turn_ref.1, s32[32]{0:T(128)} %bin_ref.1, f32[31]{0:T(128)} %taps_ref.1, f32[256,256]{1,0:T(8,128)} %constant.2.clone.hartley_ref, bf16[4,256,256]{2,1,0:T(8,128)(2,1)} %ctf_ref.1, bf16[32,256,256]{2,1,0:T(8,128)(2,1)} %tile_ref.1, ...), custom_call_target="tpu_custom_call" | custom-call | flops 4294967296 | bytes 8388608 | tf_op jit(solution)/shard_map/filter_tiles/pallas_call | solution.py:228
  32.6 0.0 copy-start.1
  32.6 9.1 %weigh_tiles.1 = (bf16[4,2,2,6,64,256]{5,4,3,2,1,0:T(8,128)(2,1)}, f32[4,8,128]{2,1,0:T(8,128)}) custom-call(s32[32]{0:T(128)} %class_ref.1, bf16[32,256,256]{2,1,0:T(8,128)(2,1)} %get-tuple-element.9.tile_ref, bf16[4,2,2,6,64,256]{5,4,3,2,1,0:T(8,128)(2,1)} %get-tuple-element.10.refs_ref), custom_call_target="tpu_custom_call" | custom-call | tf_op jit(solution)/shard_map/weigh_tiles/pallas_call | solution.py:367
  41.7 0.0 copy-done.1
  41.7 0.0 copy-start
  41.7 1.9 %copy-done = bf16[4,2,2,6,64,256]{5,4,3,2,1,0:T(8,128)(2,1)S(1)} copy-done((bf16[4,2,2,6,64,256]{5,4,3,2,1,0:T(8,128)(2,1)S(1)}, bf16[4,2,2,6,64,256]{5,4,3,2,1,0:T(8,128)(2,1)}, u32[]{:S(2)}) %copy-start) | copy-done | bytes 3145752
  43.6 0.0 copy-start.2
  43.6 0.7 copy-done.2
  44.3 26.6 %reduce_update.1 = f32[6,64,256]{2,1,0:T(8,128)S(1)} custom-call(bf16[4,2,2,6,64,256]{5,4,3,2,1,0:T(8,128)(2,1)S(1)} %copy-done, f32[4,8,128]{2,1,0:T(8,128)S(1)} %copy-done.2, bf16[6,64,256]{2,1,0:T(8,128)(2,1)S(1)} %copy-done.1), custom_call_target="tpu_custom_call" | custom-call | tf_op jit(solution)/shard_map/reduce_update/pallas_call | solution.py:477
  71.0 0.7 %copy.10 = f32[6,64,256]{2,1,0:T(8,128)} copy(f32[6,64,256]{2,1,0:T(8,128)S(1)} %reduce_update.1) | data formatting | bytes 786432
Async XLA Ops:
  32.6 9.1 %copy-start.1 = (bf16[6,64,256]{2,1,0:T(8,128)(2,1)S(1)}, bf16[6,64,256]{2,1,0:T(8,128)(2,1)}, u32[]{:S(2)}) copy-start(bf16[6,64,256]{2,1,0:T(8,128)(2,1)} %own_ref.1) | copy-start | bytes 589828
  41.7 1.9 %copy-start = (bf16[4,2,2,6,64,256]{5,4,3,2,1,0:T(8,128)(2,1)S(1)}, bf16[4,2,2,6,64,256]{5,4,3,2,1,0:T(8,128)(2,1)}, u32[]{:S(2)}) copy-start(bf16[4,2,2,6,64,256]{5,4,3,2,1,0:T(8,128)(2,1)} %get-tuple-element.11.sum_ref) | copy-start | bytes 9437188
  43.6 0.7 %copy-start.2 = (f32[4,8,128]{2,1,0:T(8,128)S(1)}, f32[4,8,128]{2,1,0:T(8,128)}, u32[]{:S(2)}) copy-start(f32[4,8,128]{2,1,0:T(8,128)} %get-tuple-element.12.weight_ref) | copy-start | bytes 49156

commit v6 on v5

--- a/solution.py
+++ b/solution.py
@@ -184,14 +184,14 @@
 
     for at, stage in stages[1:]:
 
-        @pl.when(step == jnp.minimum(at, steps - 1))
+        @pl.when(step == jnp.minimum((at + 1) // 2, steps - 1))
         def _(stage=stage):
             stage()
 
 
 def filter_tiles(particles, rotation, defocus, filter_taps, ctf_table, references, gather):
     count, tile_len, _ = particles.shape
-    batch = math.gcd(count, 2)
+    batch = math.gcd(count, 4)
     hartley = jnp.asarray(hartley_table(tile_len))
     square = (tile_len, tile_len)
     in_specs = [pl.BlockSpec(memory_space=pltpu.SMEM)] * 3 + [

time: 72.9 us -> 73 us (level); the launches traced: 71.7 us -> 72.8 us
  Pallas kernels: 68.3 us -> 69.4 us
    pallas_call x1, Pallas kernels: 26.6 us -> 28.7 us  [reduce_update(): pl.pallas_call(reduce_kernel, out_shape=jax.ShapeDtypeStruct(references.s...]
    pallas_call x1, Pallas kernels: 32.6 us -> 31.6 us  [filter_tiles(): pl.pallas_call(filter_kernel, grid=(count // batch,), in_specs=in_specs,...]
where the time goes in v6:
time: 73 us; the launch traced here: 72.8 us
  Pallas kernels  69.4 us (95%)
  local copies, waits for them, and re-layouts  3.36 us (5%)
    pallas_call x1, Pallas kernels, filter_tiles(): pl.pallas_call(filter_kernel, grid=(count // batch,), in_specs=in_specs,...  31.6 us
    pallas_call x1, Pallas kernels, reduce_update(): pl.pallas_call(reduce_kernel, out_shape=jax.ShapeDtypeStruct(references.s...  28.7 us
    pallas_call x1, Pallas kernels, weigh(): pl.pallas_call(weigh_kernel, grid_spec=grid_spec, out_shape=[jax.ShapeDty...  9.11 us
    unnamed x7, local copies, waits for them, and re-layouts  3.36 us

profile of v6, /device:TPU:0, one launch (start us, length us, event | category | flops | bytes accessed | tf_op | source)
XLA Modules:
  0.0 72.8 jit_solution(4094641508954642547)
XLA Ops:
  0.0 31.6 %filter_tiles.1 = (bf16[32,256,256]{2,1,0:T(8,128)(2,1)}, bf16[4,2,2,6,64,256]{5,4,3,2,1,0:T(8,128)(2,1)}) custom-call(s32[32]{0:T(128)} %turn_ref.1, s32[32]{0:T(128)} %bin_ref.1, f32[31]{0:T(128)} %taps_ref.1, f32[256,256]{1,0:T(8,128)} %constant.2.clone.hartley_ref, bf16[4,256,256]{2,1,0:T(8,128)(2,1)} %ctf_ref.1, bf16[32,256,256]{2,1,0:T(8,128)(2,1)} %tile_ref.1, ...), custom_call_target="tpu_custom_call" | custom-call | flops 4294967296 | bytes 8388608 | tf_op jit(solution)/shard_map/filter_tiles/pallas_call | solution.py:228
  31.6 0.0 copy-start.1
  31.6 9.1 %weigh_tiles.1 = (bf16[4,2,2,6,64,256]{5,4,3,2,1,0:T(8,128)(2,1)}, f32[4,8,128]{2,1,0:T(8,128)}) custom-call(s32[32]{0:T(128)} %class_ref.1, bf16[32,256,256]{2,1,0:T(8,128)(2,1)} %get-tuple-element.9.tile_ref, bf16[4,2,2,6,64,256]{5,4,3,2,1,0:T(8,128)(2,1)} %get-tuple-element.10.refs_ref), custom_call_target="tpu_custom_call" | custom-call | tf_op jit(solution)/shard_map/weigh_tiles/pallas_call | solution.py:367
  40.7 0.0 copy-done.1
  40.7 0.0 copy-start
  40.7 1.9 %copy-done = bf16[4,2,2,6,64,256]{5,4,3,2,1,0:T(8,128)(2,1)S(1)} copy-done((bf16[4,2,2,6,64,256]{5,4,3,2,1,0:T(8,128)(2,1)S(1)}, bf16[4,2,2,6,64,256]{5,4,3,2,1,0:T(8,128)(2,1)}, u32[]{:S(2)}) %copy-start) | copy-done | bytes 3145752
  42.6 0.0 copy-start.2
  42.6 0.7 copy-done.2
  43.3 28.7 %reduce_update.1 = f32[6,64,256]{2,1,0:T(8,128)S(1)} custom-call(bf16[4,2,2,6,64,256]{5,4,3,2,1,0:T(8,128)(2,1)S(1)} %copy-done, f32[4,8,128]{2,1,0:T(8,128)S(1)} %copy-done.2, bf16[6,64,256]{2,1,0:T(8,128)(2,1)S(1)} %copy-done.1), custom_call_target="tpu_custom_call" | custom-call | tf_op jit(solution)/shard_map/reduce_update/pallas_call | solution.py:477
  72.0 0.7 %copy.10 = f32[6,64,256]{2,1,0:T(8,128)} copy(f32[6,64,256]{2,1,0:T(8,128)S(1)} %reduce_update.1) | data formatting | bytes 786432
Async XLA Ops:
  31.6 9.1 %copy-start.1 = (bf16[6,64,256]{2,1,0:T(8,128)(2,1)S(1)}, bf16[6,64,256]{2,1,0:T(8,128)(2,1)}, u32[]{:S(2)}) copy-start(bf16[6,64,256]{2,1,0:T(8,128)(2,1)} %own_ref.1) | copy-start | bytes 589828
  40.7 1.9 %copy-start = (bf16[4,2,2,6,64,256]{5,4,3,2,1,0:T(8,128)(2,1)S(1)}, bf16[4,2,2,6,64,256]{5,4,3,2,1,0:T(8,128)(2,1)}, u32[]{:S(2)}) copy-start(bf16[4,2,2,6,64,256]{5,4,3,2,1,0:T(8,128)(2,1)} %get-tuple-element.11.sum_ref) | copy-start | bytes 9437188
  42.6 0.7 copy-start.2
